TPU v7x, 32 devices: a whole 2x2x4 slice. The times are simulated.
32 devices in a mesh: row: 4 (over y, x), col: 8 (over z, core).
Axes of the slice: x: 2, y: 2, z: 4, core: 2. Of those that a mesh axis runs over, the one named last changes fastest.
Arguments:
- factor_tiles: float32 [8, 512, 4, 1024], P(None, 'row', None, 'col'), may hold values from -40 to 40, as said below
Outputs:
- rotated: float32 [4096, 4096], P(None, ('row', 'col'))
Inputs may be any that keep to these rules, and one draw needn't show every extreme that they name: `factor_tiles`: upper triangular: entries below the diagonal are zero, entries on it are positive.
All inputs are finite; a program needn't handle non-finite values.
Results may differ from a plain program's by a relative error of at most 0.0003.
Values sent between devices are 32-bit elements; how exact they have to be, the bound alone decides.
No kernel may reach another device: no remote copies, remote signals or barrier semaphores. Data moves between devices by JAX's collectives and lax.ppermute only.
A program may use at most 128 MiB of HBM per device.

v0:
```python
import functools

import jax
import jax.numpy as jnp
from jax import lax
from jax.experimental import pallas as pl
from jax.experimental.pallas import tpu as pltpu
from jax.sharding import PartitionSpec as P

LOGB = 7
OUTER = 4
INNER = 8
LANES = 128
SUBLANES = 8
SPAN = 512
DEPTH = 2048
UNROLLED = 4096
UNITS = 32
NEAR_CUTS = (10, 22)
FAR_CUTS = (16, 24)
LAST_CUTS = (18, 26)
PIECES = 2

damping_ratio = 0.01
spare_bytes = 2048


def partner_columns(value, stride):
    if 2 * stride == value.shape[-1]:
        return pltpu.roll(value, stride, 1)
    column = lax.broadcasted_iota(jnp.int32, value.shape, 1)
    return jnp.take_along_axis(value, jnp.bitwise_xor(column, stride), axis=1)


def partner_rows(value, stride):
    order = value.shape[0]
    if stride >= 8:
        pieces = [value[start : start + stride] for start in range(0, order, stride)]
        return jnp.concatenate([pieces[place ^ 1] for place in range(len(pieces))], axis=0)
    row = lax.broadcasted_iota(jnp.int32, value.shape, 0)
    is_tail = jnp.bitwise_and(row, stride) != 0
    return jnp.where(is_tail, pltpu.roll(value, stride, 0), pltpu.roll(value, order - stride, 0))


def turn_of(own, other, cross):
    gap = own - other
    total = own + other
    base = gap * gap + damping_ratio * total * total
    tangent = jnp.where(base > 0.0, 2.0 * cross * gap / jnp.where(base > 0.0, base, 1.0), 0.0)
    inverse = lax.rsqrt(1.0 + tangent * tangent)
    square = 0.5 + 0.5 * inverse
    root = lax.rsqrt(square)
    return square * root, 0.5 * tangent * inverse * root


def inner_solve(*grams):
    shape = grams[0].shape
    row = lax.broadcasted_iota(jnp.int32, shape, 0)
    column = lax.broadcasted_iota(jnp.int32, shape, 1)
    mixed = jnp.bitwise_xor(row, column)

    def line_of(lines, place):
        return jnp.broadcast_to(lines[place : place + 1], (SUBLANES, shape[1]))

    def spread(line):
        return jnp.broadcast_to(line[None], (shape[0] // SUBLANES, *line.shape)).reshape(shape)

    state = []
    for gram in grams:
        lines = gram
        for bit in range(LOGB):
            is_set = jnp.bitwise_and(column, 2**bit) != 0
            lines = jnp.where(is_set, partner_rows(lines, 2**bit), lines)
        start = jnp.where(row == column, 1.0, 0.0).astype(jnp.float32)
        state.append((lines, line_of(lines, 0), start))
    for step in range(INNER):
        stride = 2 ** ((LOGB - 1 - step) % LOGB)
        after = []
        for lines, own, turned in state:
            other = partner_columns(own, stride)
            cross = line_of(lines, stride)
            cosine, sine = turn_of(own, other, cross)
            own = cosine * (cosine * own + 2.0 * sine * cross) + sine * sine * other
            cosine, sine = spread(cosine), spread(sine)
            turned = turned * cosine + partner_columns(turned, stride) * sine
            if step + 1 < INNER:
                across = partner_rows(partner_columns(lines, stride), stride)
                lines = lines * cosine + across * sine
                cos_mixed = jnp.take_along_axis(cosine, mixed, axis=1)
                sin_mixed = jnp.take_along_axis(sine, mixed, axis=1)
                lines = lines * cos_mixed + partner_rows(lines, stride) * sin_mixed
            after.append((lines, own, turned))
        state = after
    return [turned.T for _, _, turned in state]


def three_parts(value):
    high = value.astype(jnp.bfloat16)
    rest = value - high.astype(jnp.float32)
    middle = rest.astype(jnp.bfloat16)
    return high, middle, (rest - middle.astype(jnp.float32)).astype(jnp.bfloat16)


def split_store(split_ref, value, start, lane):
    order = split_ref.shape[0] // 3
    rows, lanes = value.shape
    high, middle, low = three_parts(value)
    for place, part in enumerate((middle, high, low)):
        split_ref[pl.ds(place * order + start, rows), pl.ds(lane, lanes)] = part


def gram_of(split_ref):
    order = split_ref.shape[0] // 3
    total = split_ref.shape[1]

    def body(place, acc):
        lanes = pl.ds(pl.multiple_of(place * DEPTH, DEPTH), DEPTH)
        return acc + lax.dot_general(
            split_ref[:, lanes],
            split_ref[: 2 * order, lanes],
            (((1,), (1,)), ((), ())),
            preferred_element_type=jnp.float32,
        )

    acc = lax.fori_loop(0, total // DEPTH, body, jnp.zeros((3 * order, 2 * order), jnp.float32))
    outer = acc[2 * order :, order:]
    inner = acc[:order, order:] + acc[order : 2 * order, :order] + acc[:order, :order]
    return acc[order : 2 * order, order:] + (inner + (outer + outer.T))


def product(turned, split_ref, lanes, terms=6):
    order = split_ref.shape[0] // 3
    rows = turned.shape[0]
    high, middle, low = three_parts(turned)

    def dot(weights, start):
        return lax.dot_general(
            jnp.concatenate([jnp.concatenate(pair, axis=1) for pair in weights], axis=0),
            split_ref[start : start + 2 * order, lanes],
            (((1,), (0,)), ((), ())),
            preferred_element_type=jnp.float32,
        )

    both = dot(((high, high), (middle, middle)), 0)
    if terms == 4:
        return both[:rows] + both[rows:]
    return both[:rows] + (both[rows:] + dot(((low, high),), order))


def spans(length, body):
    whole = length // SPAN * SPAN
    if length <= UNROLLED:
        for lane in range(0, whole, SPAN):
            body(lane, SPAN)
    else:

        def step(place, carry):
            body(pl.multiple_of(place * SPAN, SPAN), SPAN)
            return carry

        lax.fori_loop(0, length // SPAN, step, 0)
    if whole < length:
        body(whole, length - whole)


def load_rows(split_ref, refs, start):
    done = 0
    for ref in refs:

        def body(lane, size):
            split_store(split_ref, ref[:, pl.ds(lane, size)], start, done + lane)

        spans(ref.shape[1], body)
        done += ref.shape[1]


def cuts_of(refs):
    cuts = [0]
    for ref in refs:
        cuts.append(cuts[-1] + ref.shape[1])
    return cuts


def send_out(turned, split_ref, first_refs, second_refs, swap, terms=6):
    half = split_ref.shape[0] // 6
    swapped = jnp.concatenate([turned[half:], turned[:half]], axis=0)
    arranged = jnp.where(swap, swapped, turned)
    first_cuts, second_cuts = cuts_of(first_refs), cuts_of(second_refs)
    cuts = sorted(set(first_cuts + second_cuts))
    for begin, end in zip(cuts[:-1], cuts[1:]):
        first = max(place for place, cut in enumerate(first_cuts) if cut <= begin)
        second = max(place for place, cut in enumerate(second_cuts) if cut <= begin)
        first_lane, second_lane = begin - first_cuts[first], begin - second_cuts[second]

        def body(lane, size):
            lines = product(arranged, split_ref, pl.ds(begin + lane, size), terms)
            first_refs[first][:, pl.ds(first_lane + lane, size)] = lines[:half]
            second_refs[second][:, pl.ds(second_lane + lane, size)] = lines[half:]

        spans(end - begin, body)


def run_of(column, row, row_count, column_count):
    last = jnp.where(row == row_count - 1, row, row_count - 2 - row)
    odd = jnp.where(column == column_count - 1, last, row_count - 1 - row)
    return jnp.where(jnp.bitwise_and(column, 1) == 0, row, odd)


def hosted_slot():
    column, columns = lax.axis_index("col"), lax.axis_size("col")
    run = run_of(column, lax.axis_index("row"), lax.axis_size("row"), columns)
    return run * columns + column


def slot_count():
    return lax.axis_size("row") * lax.axis_size("col")


def prepare_kernel(order, in_ref, *refs):
    count = lax.axis_size("row")
    out_refs, buffer, ready = refs[:-2], refs[-2], refs[-1]
    cycles, rows = in_ref.shape[0], in_ref.shape[1] // count
    copies = [
        pltpu.make_async_copy(in_ref.at[cycle], buffer.at[cycle], ready.at[cycle])
        for cycle in range(cycles)
    ]
    for copy in copies:
        copy.start()
    me = lax.axis_index("row")
    column, columns = lax.axis_index("col"), lax.axis_size("col")
    per_piece = cycles // PIECES
    for cycle, copy in enumerate(copies):
        copy.wait()
        piece, place = divmod(cycle, per_piece)
        for offset in range(count):
            tile = run_of(column, jnp.bitwise_xor(me, offset), count, columns)
            out_ref = out_refs[order.index((offset, piece))]
            out_ref[:, place * rows : (place + 1) * rows] = buffer[
                cycle, pl.ds(tile, rows, stride=count), :
            ].T


def odd_chip(slot):
    return jnp.bitwise_and(slot // 2, 1)


def first_kernel(order, near_count, *refs):
    chunk_refs, out_refs, split_ref = refs[: len(order)], refs[len(order) : -1], refs[-1]
    me, count = lax.axis_index("row"), lax.axis_size("row")
    total = split_ref.shape[1]
    rows = split_ref.shape[0] // 3
    per_piece = total // (PIECES * count * rows)
    for (offset, piece), chunk_ref in zip(order, chunk_refs):
        peer = jnp.bitwise_xor(me, offset)
        for place in range(per_piece):
            lane = ((piece * per_piece + place) * count + peer) * rows
            split_store(
                split_ref,
                chunk_ref[:, place * rows : (place + 1) * rows],
                0,
                pl.multiple_of(lane, rows),
            )
    (turned,) = inner_solve(gram_of(split_ref))
    slot = hosted_slot()
    bottom_first = jnp.logical_or(odd_chip(slot) == 1, slot == 0)
    send_out(turned, split_ref, out_refs[-near_count:], out_refs[:-near_count], bottom_first)


def middle_kernel(near_count, *refs):
    sizes = len(LAST_CUTS) + 1
    near_ref, far_ref = refs[-2:]
    off_outs, on_outs = refs[-2 - 2 * sizes : -2 - sizes], refs[-2 - sizes : -2]
    halves = refs[: -2 - 2 * sizes]
    in_refs, own_refs = halves[: len(halves) // 2], halves[len(halves) // 2 :]
    far_in, near_in = in_refs[:-near_count], in_refs[-near_count:]
    second, first = own_refs[:-near_count], own_refs[-near_count:]
    slot, slots = hosted_slot(), slot_count()
    half = off_outs[0].shape[0]
    odd = odd_chip(slot)
    at_end = jnp.logical_or(slot == 0, slot == slots - 1).astype(jnp.int32)
    near_own = pl.multiple_of(odd * half, half)
    near_other = pl.multiple_of((1 - odd) * half, half)
    far_own = pl.multiple_of(jnp.bitwise_xor(1 - odd, at_end) * half, half)
    far_other = pl.multiple_of(jnp.bitwise_xor(odd, at_end) * half, half)
    load_rows(near_ref, first, near_own)
    load_rows(near_ref, near_in, near_other)
    load_rows(far_ref, second, far_own)
    load_rows(far_ref, far_in, far_other)
    near, far = inner_solve(gram_of(near_ref), gram_of(far_ref))
    near_half = jnp.where(odd == 0, near[half:], near[:half])
    flipped = jnp.logical_or(slot == 1, slot == slots - 1)
    far_bottom = jnp.logical_xor(odd == 1, flipped)
    far_half = jnp.where(far_bottom, far[half:], far[:half])

    def body(lane, size):
        near_lines = product(near_half, near_ref, pl.ds(lane, size))
        far_lines = product(far_half, far_ref, pl.ds(lane, size))
        split_store(near_ref, near_lines, near_other, lane)
        split_store(near_ref, far_lines, near_own, lane)

    spans(near_ref.shape[1], body)
    (turned,) = inner_solve(gram_of(near_ref))
    swap = jnp.logical_and(jnp.bitwise_and(slot, 1) == 0, slot != 0)
    send_out(turned, near_ref, off_outs, on_outs, swap, terms=4)


def last_kernel(*refs):
    out_ref, split_ref, buffer, done = refs[-4:]
    sizes = (len(refs) - 4) // 2
    off_in, on_in = refs[:sizes], refs[sizes:-4]
    half = off_in[0].shape[0]
    odd = jnp.bitwise_and(lax.axis_index("col"), 1)
    load_rows(split_ref, off_in, pl.multiple_of(odd * half, half))
    load_rows(split_ref, on_in, pl.multiple_of((1 - odd) * half, half))
    (turned,) = inner_solve(gram_of(split_ref))
    total = split_ref.shape[1]

    def copy_of(lane):
        rows = pl.ds(lane, SPAN)
        return pltpu.make_async_copy(buffer.at[rows], out_ref.at[rows], done.at[lane // SPAN])

    def body(lane, size):
        lines = product(turned, split_ref, pl.ds(lane, size), terms=4)
        for place in range(0, size, LANES):
            buffer[pl.ds(lane + place, LANES), :] = lines[:, place : place + LANES].T
        copy_of(lane).start()

    spans(total, body)
    spans(total, lambda lane, size: copy_of(lane).wait())


def in_vmem(count):
    return [pl.BlockSpec(memory_space=pltpu.VMEM)] * count


def host_of(slot, row_count, column_count):
    run, column = divmod(slot, column_count)
    row = run
    if column == column_count - 1:
        row = run if run == row_count - 1 else row_count - 2 - run
    elif column % 2:
        row = row_count - 1 - run
    return row * column_count + column


def peer_pairs(offset, first_row, width, row_count, column_count):
    pairs = []
    for row in range(row_count):
        for column in range(column_count):
            peer = (row ^ offset) * column_count + column
            slot = host_of(peer, row_count, column_count)
            if (slot + 1) * width > first_row:
                pairs.append((row * column_count + column, peer))
    return pairs


def swap_pairs(first_row, width, row_count, column_count):
    slots = row_count * column_count
    near_pairs, far_pairs = [], []
    for slot in range(slots):
        if (slot + 1) * width <= first_row:
            continue
        source = host_of(slot, row_count, column_count)
        step = -2 if slot // 2 % 2 else 2
        near_pairs.append((source, host_of(slot + step, row_count, column_count)))
        target = slot - step if 0 <= slot - step < slots else slot ^ 1
        far_pairs.append((source, host_of(target, row_count, column_count)))
    return near_pairs, far_pairs


def last_pairs(first_row, width, row_count, column_count):
    slots = row_count * column_count
    off_pairs, on_pairs = [], []
    for slot in range(slots):
        if (slot + OUTER - 1) * width > first_row:
            target = slot + 1 if slot % 2 else slot - 1
            source = host_of(slot, row_count, column_count)
            off_pairs.append((source, target if 0 <= target < slots else slot))
            on_pairs.append((source, slot ^ 1))
    return off_pairs, on_pairs


def per_device(factor_tiles):
    cycles, rows, tiles, width = factor_tiles.shape
    count, columns = lax.axis_size("row"), lax.axis_size("col")
    half = width // 2
    length = cycles * rows * count
    axes = ("row", "col")
    split_bytes, spare = 6 * width * length, spare_bytes * length
    params = pltpu.CompilerParams(vmem_limit_bytes=split_bytes + spare)
    more_params = pltpu.CompilerParams(vmem_limit_bytes=2 * split_bytes + spare)
    split = pltpu.VMEM((3 * width, length), jnp.bfloat16)

    order = [(peer, part) for peer in range(tiles - 1, -1, -1) for part in range(PIECES - 1, -1, -1)]
    pieces = len(order)
    chunks = pl.pallas_call(
        functools.partial(prepare_kernel, order),
        in_specs=[pl.BlockSpec(memory_space=pltpu.HBM)],
        out_specs=in_vmem(pieces),
        out_shape=[jax.ShapeDtypeStruct((width, cycles * rows // PIECES), jnp.float32)] * pieces,
        scratch_shapes=[
            pltpu.VMEM((cycles, rows * tiles, width), jnp.float32),
            pltpu.SemaphoreType.DMA((cycles,)),
        ],
        compiler_params=params,
        name="prepare",
    )(factor_tiles.reshape(cycles, rows * tiles, width))
    received = list(chunks)
    for place, (offset, piece) in enumerate(order):
        if offset:
            pairs = peer_pairs(offset, piece * (length // PIECES), width, count, columns)
            received[place] = lax.ppermute(chunks[place], axes, pairs)

    unit = length // UNITS
    near_starts = [0] + [cut * unit for cut in NEAR_CUTS]
    far_starts = [0] + [cut * unit for cut in FAR_CUTS]
    near_count = len(near_starts)
    halves = [
        jax.ShapeDtypeStruct((half, end - start), jnp.float32)
        for starts in (far_starts, near_starts)
        for start, end in zip(starts, starts[1:] + [length])
    ]
    moved = pl.pallas_call(
        functools.partial(first_kernel, order, near_count),
        in_specs=in_vmem(pieces),
        out_specs=in_vmem(len(halves)),
        out_shape=halves,
        scratch_shapes=[split],
        compiler_params=params,
        name="first_round",
    )(*received)
    far, near = list(moved[:-near_count]), list(moved[-near_count:])

    def swapped(value, first_row, side):
        return lax.ppermute(value, axes, swap_pairs(first_row, width, count, columns)[side])

    far = [swapped(value, start, 1) for value, start in zip(far, far_starts)]
    near = [swapped(value, start, 0) for value, start in zip(near, near_starts)]
    last_starts = [0] + [cut * unit for cut in LAST_CUTS]
    sizes = len(last_starts)
    last_halves = [
        jax.ShapeDtypeStruct((half, end - start), jnp.float32)
        for start, end in zip(last_starts, last_starts[1:] + [length])
    ]
    last = pl.pallas_call(
        functools.partial(middle_kernel, near_count),
        in_specs=in_vmem(2 * len(halves)),
        out_specs=in_vmem(2 * sizes),
        out_shape=last_halves * 2,
        scratch_shapes=[split] * 2,
        compiler_params=more_params,
        name="middle_rounds",
    )(*far, *near, *moved)
    off, on = list(last[:sizes]), list(last[sizes:])
    for place, start in enumerate(last_starts):
        off_pairs, on_pairs = last_pairs(start, width, count, columns)
        off[place] = lax.ppermute(off[place], axes, off_pairs)
        on[place] = lax.ppermute(on[place], axes, on_pairs)
    return pl.pallas_call(
        last_kernel,
        in_specs=in_vmem(2 * sizes),
        out_specs=pl.BlockSpec(memory_space=pltpu.HBM),
        out_shape=jax.ShapeDtypeStruct((length, width), jnp.float32),
        scratch_shapes=[
            split,
            pltpu.VMEM((length, width), jnp.float32),
            pltpu.SemaphoreType.DMA((length // SPAN,)),
        ],
        compiler_params=params,
        name="last_round",
    )(*off, *on)


def solution(mesh):
    return jax.shard_map(
        per_device,
        mesh=mesh,
        in_specs=(P(None, "row", None, "col"),),
        out_specs=P(None, ("row", "col")),
        check_vma=False,
    )
```

profile of v0, /device:TPU:22, one launch (start us, length us, event | category | flops | bytes accessed | tf_op | source)
XLA Modules:
  0.0 108.6 jit_solution(9509283645959074493)
XLA Ops:
  4.2 3.6 %collective-permute-start.1 = (f32[128,512]{1,0:T(8,128)S(1)}, f32[128,512]{1,0:T(8,128)S(1)}, u32[]{:S(2)}, u32[]{:S(2)}) collective-permute-start(f32[128,512]{1,0:T(8,128)S(1)} %get-tuple-element.26), channel_id=1, source_target_pairs={{0,24},{1,25},{2,26},{3,27},{4,28},{5,29},{6,30},{7,31},{8,16},{9,... | collective-permute-start | bytes 786440 | tf_op jit(solution)/shard_map/ppermute | solution.py:412
  9.1 2.7 %collective-permute-start.3 = (f32[128,512]{1,0:T(8,128)S(1)}, f32[128,512]{1,0:T(8,128)S(1)}, u32[]{:S(2)}, u32[]{:S(2)}) collective-permute-start(f32[128,512]{1,0:T(8,128)S(1)} %get-tuple-element.28), channel_id=1, source_target_pairs={{0,16},{1,17},{2,18},{3,19},{4,20},{5,21},{6,22},{7,23},{8,24},{9,... | collective-permute-start | bytes 786440 | tf_op jit(solution)/shard_map/ppermute | solution.py:412
  11.8 2.4 %collective-permute-start.4 = (f32[128,512]{1,0:T(8,128)S(1)}, f32[128,512]{1,0:T(8,128)S(1)}, u32[]{:S(2)}, u32[]{:S(2)}) collective-permute-start(f32[128,512]{1,0:T(8,128)S(1)} %get-tuple-element.29), channel_id=1, source_target_pairs={{1,9},{3,11},{5,13},{9,1},{11,3},{13,5},{15,7},{16,24},{18,26},{20... | collective-permute-start | bytes 786440 | tf_op jit(solution)/shard_map/ppermute | solution.py:412
  15.8 2.9 %collective-permute-done.1.refs_1_ = f32[128,512]{1,0:T(8,128)S(1)} collective-permute-done((f32[128,512]{1,0:T(8,128)S(1)}, f32[128,512]{1,0:T(8,128)S(1)}, u32[]{:S(2)}, u32[]{:S(2)}) %collective-permute-start.1) | collective-permute-done | bytes 262176 | tf_op jit(solution)/shard_map/ppermute | solution.py:412
  18.8 3.7 %collective-permute-done.2.refs_2_ = f32[128,512]{1,0:T(8,128)S(1)} collective-permute-done((f32[128,512]{1,0:T(8,128)S(1)}, f32[128,512]{1,0:T(8,128)S(1)}, u32[]{:S(2)}, u32[]{:S(2)}) %collective-permute-start.2) | collective-permute-done | bytes 262176 | tf_op jit(solution)/shard_map/ppermute | solution.py:412
  22.5 2.8 %collective-permute-done.3.refs_3_ = f32[128,512]{1,0:T(8,128)S(1)} collective-permute-done((f32[128,512]{1,0:T(8,128)S(1)}, f32[128,512]{1,0:T(8,128)S(1)}, u32[]{:S(2)}, u32[]{:S(2)}) %collective-permute-start.3) | collective-permute-done | bytes 262176 | tf_op jit(solution)/shard_map/ppermute | solution.py:412
  25.3 4.6 %first_round.1 = (f32[64,2048]{1,0:T(8,128)S(1)}, f32[64,1024]{1,0:T(8,128)S(1)}, f32[64,1024]{1,0:T(8,128)S(1)}, f32[64,1280]{1,0:T(8,128)S(1)}, f32[64,1536]{1,0:T(8,128)S(1)}, /*index=5*/f32[64,1280]{1,0:T(8,128)S(1)}) custom-call(f32[128,512]{1,0:T(8,128)S(1)} %collective-permute-done.refs_0_, f32[128,512]{1,0:T(8,128)S(1)} %collective-permute-done.1.refs_1_, ...), custom_call_target="tpu_custom_call" | custom-call | tf_op jit(solution)/shard_map/first_round/pallas_call | solution.py:423
  29.9 2.4 %collective-permute-start.7 = (f32[64,1024]{1,0:T(8,128)S(1)}, f32[64,1024]{1,0:T(8,128)S(1)}, u32[]{:S(2)}, u32[]{:S(2)}) collective-permute-start(f32[64,1024]{1,0:T(8,128)S(1)} %get-tuple-element.34.refs_7_), channel_id=1, source_target_pairs={{16,14},{9,15},{18,20},{11,13},{20,18},{13,11},{22,24},{7,1},{24,2... | collective-permute-start | bytes 786440 | tf_op jit(solution)/shard_map/ppermute | solution.py:435
  33.9 7.3 %collective-permute-start.10 = (f32[64,1536]{1,0:T(8,128)S(1)}, f32[64,1536]{1,0:T(8,128)S(1)}, u32[]{:S(2)}, u32[]{:S(2)}) collective-permute-start(f32[64,1536]{1,0:T(8,128)S(1)} %get-tuple-element.37.refs_10_), channel_id=1, source_target_pairs={{10,8},{19,17},{12,14},{21,15},{14,12},{15,21},{16,18},{9,11},{18,... | collective-permute-start | bytes 1179656 | tf_op jit(solution)/shard_map/ppermute | solution.py:435
  41.3 3.9 %collective-permute-start.11 = (f32[64,1280]{1,0:T(8,128)S(1)}, f32[64,1280]{1,0:T(8,128)S(1)}, u32[]{:S(2)}, u32[]{:S(2)}) collective-permute-start(f32[64,1280]{1,0:T(8,128)S(1)} %get-tuple-element.38.refs_11_), channel_id=1, source_target_pairs={{22,20},{7,13},{24,26},{1,3},{26,24},{3,1},{28,30},{5,31},{30,28},... | collective-permute-start | bytes 983048 | tf_op jit(solution)/shard_map/ppermute | solution.py:435
  45.2 2.8 %collective-permute-done.7.refs_1_ = f32[64,1024]{1,0:T(8,128)S(1)} collective-permute-done((f32[64,1024]{1,0:T(8,128)S(1)}, f32[64,1024]{1,0:T(8,128)S(1)}, u32[]{:S(2)}, u32[]{:S(2)}) %collective-permute-start.7) | collective-permute-done | bytes 262176 | tf_op jit(solution)/shard_map/ppermute | solution.py:435
  47.9 1.9 %collective-permute-start.8 = (f32[64,1024]{1,0:T(8,128)S(1)}, f32[64,1024]{1,0:T(8,128)S(1)}, u32[]{:S(2)}, u32[]{:S(2)}) collective-permute-start(f32[64,1024]{1,0:T(8,128)S(1)} %get-tuple-element.35.refs_8_), channel_id=1, source_target_pairs={{24,22},{1,7},{26,28},{3,5},{28,26},{5,3},{30,31},{31,30}} | collective-permute-start | bytes 786440 | tf_op jit(solution)/shard_map/ppermute | solution.py:435
  49.8 6.5 %collective-permute-done.8.refs_2_ = f32[64,1024]{1,0:T(8,128)S(1)} collective-permute-done((f32[64,1024]{1,0:T(8,128)S(1)}, f32[64,1024]{1,0:T(8,128)S(1)}, u32[]{:S(2)}, u32[]{:S(2)}) %collective-permute-start.8) | collective-permute-done | bytes 262176 | tf_op jit(solution)/shard_map/ppermute | solution.py:435
  56.4 1.7 %collective-permute-done.9.refs_3_ = f32[64,1280]{1,0:T(8,128)S(1)} collective-permute-done((f32[64,1280]{1,0:T(8,128)S(1)}, f32[64,1280]{1,0:T(8,128)S(1)}, u32[]{:S(2)}, u32[]{:S(2)}) %collective-permute-start.9) | collective-permute-done | bytes 327712 | tf_op jit(solution)/shard_map/ppermute | solution.py:435
  58.1 6.4 %collective-permute-done.11.refs_5_ = f32[64,1280]{1,0:T(8,128)S(1)} collective-permute-done((f32[64,1280]{1,0:T(8,128)S(1)}, f32[64,1280]{1,0:T(8,128)S(1)}, u32[]{:S(2)}, u32[]{:S(2)}) %collective-permute-start.11) | collective-permute-done | bytes 327712 | tf_op jit(solution)/shard_map/ppermute | solution.py:435
  64.5 10.7 %middle_rounds.1 = (f32[64,2304]{1,0:T(8,128)S(1)}, f32[64,1024]{1,0:T(8,128)S(1)}, f32[64,768]{1,0:T(8,128)S(1)}, f32[64,2304]{1,0:T(8,128)S(1)}, f32[64,1024]{1,0:T(8,128)S(1)}, /*index=5*/f32[64,768]{1,0:T(8,128)S(1)}) custom-call(f32[64,2048]{1,0:T(8,128)S(1)} %collective-permute-done.6.refs_0_, f32[64,1024]{1,0:T(8,128)S(1)} %collective-permute-done.7.refs_1_, ...), custom_call_target="tpu_custom_call" | custom-call | tf_op jit(solution)/shard_map/middle_rounds/pallas_call | solution.py:445
  75.2 1.9 %collective-permute-start.12 = (f32[64,2304]{1,0:T(8,128)S(1)}, f32[64,2304]{1,0:T(8,128)S(1)}, u32[]{:S(2)}, u32[]{:S(2)}) collective-permute-start(f32[64,2304]{1,0:T(8,128)S(1)} %get-tuple-element.39), channel_id=1, source_target_pairs={{0,0},{25,2},{2,1},{27,4},{4,3},{29,6},{6,5},{23,8},{8,7},{17,10},... | collective-permute-start | bytes 1769480 | tf_op jit(solution)/shard_map/ppermute | solution.py:457
  77.2 2.5 %collective-permute-start.14 = (f32[64,768]{1,0:T(8,128)S(1)}, f32[64,768]{1,0:T(8,128)S(1)}, u32[]{:S(2)}, u32[]{:S(2)}) collective-permute-start(f32[64,768]{1,0:T(8,128)S(1)} %get-tuple-element.41), channel_id=1, source_target_pairs={{24,23},{1,26},{26,25},{3,28},{28,27},{5,30},{30,29},{31,31}} | collective-permute-start | bytes 589832 | tf_op jit(solution)/shard_map/ppermute | solution.py:457
  79.8 1.9 %collective-permute-start.13 = (f32[64,1024]{1,0:T(8,128)S(1)}, f32[64,1024]{1,0:T(8,128)S(1)}, u32[]{:S(2)}, u32[]{:S(2)}) collective-permute-start(f32[64,1024]{1,0:T(8,128)S(1)} %get-tuple-element.40), channel_id=1, source_target_pairs={{16,15},{9,18},{18,17},{11,20},{20,19},{13,22},{22,21},{7,24},{24,... | collective-permute-start | bytes 786440 | tf_op jit(solution)/shard_map/ppermute | solution.py:457
  81.7 1.9 %collective-permute-start.16 = (f32[64,1024]{1,0:T(8,128)S(1)}, f32[64,1024]{1,0:T(8,128)S(1)}, u32[]{:S(2)}, u32[]{:S(2)}) collective-permute-start(f32[64,1024]{1,0:T(8,128)S(1)} %get-tuple-element.43), channel_id=1, source_target_pairs={{16,17},{9,16},{18,19},{11,18},{20,21},{13,20},{22,23},{7,22},{24,... | collective-permute-start | bytes 786440 | tf_op jit(solution)/shard_map/ppermute | solution.py:458
  83.6 6.8 %collective-permute-done.14.refs_2_ = f32[64,768]{1,0:T(8,128)S(1)} collective-permute-done((f32[64,768]{1,0:T(8,128)S(1)}, f32[64,768]{1,0:T(8,128)S(1)}, u32[]{:S(2)}, u32[]{:S(2)}) %collective-permute-start.14) | collective-permute-done | bytes 196640 | tf_op jit(solution)/shard_map/ppermute | solution.py:457
  90.4 2.1 %collective-permute-start.17 = (f32[64,768]{1,0:T(8,128)S(1)}, f32[64,768]{1,0:T(8,128)S(1)}, u32[]{:S(2)}, u32[]{:S(2)}) collective-permute-start(f32[64,768]{1,0:T(8,128)S(1)} %get-tuple-element.44), channel_id=1, source_target_pairs={{24,25},{1,24},{26,27},{3,26},{28,29},{5,28},{30,31},{31,30}} | collective-permute-start | bytes 589832 | tf_op jit(solution)/shard_map/ppermute | solution.py:458
  92.5 11.0 %collective-permute-done.17.refs_5_ = f32[64,768]{1,0:T(8,128)S(1)} collective-permute-done((f32[64,768]{1,0:T(8,128)S(1)}, f32[64,768]{1,0:T(8,128)S(1)}, u32[]{:S(2)}, u32[]{:S(2)}) %collective-permute-start.17) | collective-permute-done | bytes 196640 | tf_op jit(solution)/shard_map/ppermute | solution.py:458
  103.6 4.9 %last_round.1 = f32[4096,128]{1,0:T(8,128)} custom-call(f32[64,2304]{1,0:T(8,128)S(1)} %collective-permute-done.12.refs_0_, f32[64,1024]{1,0:T(8,128)S(1)} %collective-permute-done.13.refs_1_, f32[64,768]{1,0:T(8,128)S(1)} %collective-permute-done.14.refs_2_, f32[64,2304]{1,0:T(8,128)S(1)} %collective-permute-done.15.refs_3_, ...), custom_call_target="tpu_custom_call" | custom-call | tf_op jit(solution)/shard_map/last_round/pallas_call | solution.py:459
  (18 shorter events, 8.8 us)
Async XLA Ops:
  0.0 1.6 %copy-start = (f32[8,128,4,128]{3,2,1,0:T(4,128)S(1)}, f32[8,128,4,128]{3,2,1,0:T(4,128)}, u32[]{:S(2)}) copy-start(f32[8,128,4,128]{3,2,1,0:T(4,128)} %param.1) | copy-start | bytes 6291460
  2.9 11.4 %collective-permute-start = (f32[128,512]{1,0:T(8,128)S(1)}, f32[128,512]{1,0:T(8,128)S(1)}, u32[]{:S(2)}, u32[]{:S(2)}) collective-permute-start(f32[128,512]{1,0:T(8,128)S(1)} %get-tuple-element.25), channel_id=1, source_target_pairs={{0,24},{2,26},{4,28},{6,30},{7,31},{8,16},{10,18},{12,20},{14,22},... | collective-permute-start | bytes 786440 | tf_op jit(solution)/shard_map/ppermute | solution.py:412
  4.2 14.5 %collective-permute-start.1 = (f32[128,512]{1,0:T(8,128)S(1)}, f32[128,512]{1,0:T(8,128)S(1)}, u32[]{:S(2)}, u32[]{:S(2)}) collective-permute-start(f32[128,512]{1,0:T(8,128)S(1)} %get-tuple-element.26), channel_id=1, source_target_pairs={{0,24},{1,25},{2,26},{3,27},{4,28},{5,29},{6,30},{7,31},{8,16},{9,... | collective-permute-start | bytes 786440 | tf_op jit(solution)/shard_map/ppermute | solution.py:412
  7.8 14.6 %collective-permute-start.2 = (f32[128,512]{1,0:T(8,128)S(1)}, f32[128,512]{1,0:T(8,128)S(1)}, u32[]{:S(2)}, u32[]{:S(2)}) collective-permute-start(f32[128,512]{1,0:T(8,128)S(1)} %get-tuple-element.27), channel_id=1, source_target_pairs={{0,16},{2,18},{4,20},{6,22},{8,24},{10,26},{12,28},{14,30},{15,31}... | collective-permute-start | bytes 786440 | tf_op jit(solution)/shard_map/ppermute | solution.py:412
  9.1 16.2 %collective-permute-start.3 = (f32[128,512]{1,0:T(8,128)S(1)}, f32[128,512]{1,0:T(8,128)S(1)}, u32[]{:S(2)}, u32[]{:S(2)}) collective-permute-start(f32[128,512]{1,0:T(8,128)S(1)} %get-tuple-element.28), channel_id=1, source_target_pairs={{0,16},{1,17},{2,18},{3,19},{4,20},{5,21},{6,22},{7,23},{8,24},{9,... | collective-permute-start | bytes 786440 | tf_op jit(solution)/shard_map/ppermute | solution.py:412
  11.8 13.4 %collective-permute-start.4 = (f32[128,512]{1,0:T(8,128)S(1)}, f32[128,512]{1,0:T(8,128)S(1)}, u32[]{:S(2)}, u32[]{:S(2)}) collective-permute-start(f32[128,512]{1,0:T(8,128)S(1)} %get-tuple-element.29), channel_id=1, source_target_pairs={{1,9},{3,11},{5,13},{9,1},{11,3},{13,5},{15,7},{16,24},{18,26},{20... | collective-permute-start | bytes 786440 | tf_op jit(solution)/shard_map/ppermute | solution.py:412
  14.3 11.0 %collective-permute-start.5 = (f32[128,512]{1,0:T(8,128)S(1)}, f32[128,512]{1,0:T(8,128)S(1)}, u32[]{:S(2)}, u32[]{:S(2)}) collective-permute-start(f32[128,512]{1,0:T(8,128)S(1)} %get-tuple-element.30), channel_id=1, source_target_pairs={{0,8},{1,9},{2,10},{3,11},{4,12},{5,13},{6,14},{7,15},{8,0},{9,1},... | collective-permute-start | bytes 786440 | tf_op jit(solution)/shard_map/ppermute | solution.py:412
  29.9 18.0 %collective-permute-start.7 = (f32[64,1024]{1,0:T(8,128)S(1)}, f32[64,1024]{1,0:T(8,128)S(1)}, u32[]{:S(2)}, u32[]{:S(2)}) collective-permute-start(f32[64,1024]{1,0:T(8,128)S(1)} %get-tuple-element.34.refs_7_), channel_id=1, source_target_pairs={{16,14},{9,15},{18,20},{11,13},{20,18},{13,11},{22,24},{7,1},{24,2... | collective-permute-start | bytes 786440 | tf_op jit(solution)/shard_map/ppermute | solution.py:435
  32.2 32.3 %collective-permute-start.6 = (f32[64,2048]{1,0:T(8,128)S(1)}, f32[64,2048]{1,0:T(8,128)S(1)}, u32[]{:S(2)}, u32[]{:S(2)}) collective-permute-start(f32[64,2048]{1,0:T(8,128)S(1)} %get-tuple-element.33.refs_6_), channel_id=1, source_target_pairs={{0,25},{25,0},{2,4},{27,29},{4,2},{29,27},{6,8},{23,17},{8,6},{17,... | collective-permute-start | bytes 1572872 | tf_op jit(solution)/shard_map/ppermute | solution.py:435
  33.9 30.6 %collective-permute-start.10 = (f32[64,1536]{1,0:T(8,128)S(1)}, f32[64,1536]{1,0:T(8,128)S(1)}, u32[]{:S(2)}, u32[]{:S(2)}) collective-permute-start(f32[64,1536]{1,0:T(8,128)S(1)} %get-tuple-element.37.refs_10_), channel_id=1, source_target_pairs={{10,8},{19,17},{12,14},{21,15},{14,12},{15,21},{16,18},{9,11},{18,... | collective-permute-start | bytes 1179656 | tf_op jit(solution)/shard_map/ppermute | solution.py:435
  41.2 16.9 %collective-permute-start.9 = (f32[64,1280]{1,0:T(8,128)S(1)}, f32[64,1280]{1,0:T(8,128)S(1)}, u32[]{:S(2)}, u32[]{:S(2)}) collective-permute-start(f32[64,1280]{1,0:T(8,128)S(1)} %get-tuple-element.36.refs_9_), channel_id=1, source_target_pairs={{0,2},{25,27},{2,0},{27,25},{4,6},{29,23},{6,4},{23,29},{8,10},{17... | collective-permute-start | bytes 983048 | tf_op jit(solution)/shard_map/ppermute | solution.py:435
  41.3 23.3 %collective-permute-start.11 = (f32[64,1280]{1,0:T(8,128)S(1)}, f32[64,1280]{1,0:T(8,128)S(1)}, u32[]{:S(2)}, u32[]{:S(2)}) collective-permute-start(f32[64,1280]{1,0:T(8,128)S(1)} %get-tuple-element.38.refs_11_), channel_id=1, source_target_pairs={{22,20},{7,13},{24,26},{1,3},{26,24},{3,1},{28,30},{5,31},{30,28},... | collective-permute-start | bytes 983048 | tf_op jit(solution)/shard_map/ppermute | solution.py:435
  47.9 8.4 %collective-permute-start.8 = (f32[64,1024]{1,0:T(8,128)S(1)}, f32[64,1024]{1,0:T(8,128)S(1)}, u32[]{:S(2)}, u32[]{:S(2)}) collective-permute-start(f32[64,1024]{1,0:T(8,128)S(1)} %get-tuple-element.35.refs_8_), channel_id=1, source_target_pairs={{24,22},{1,7},{26,28},{3,5},{28,26},{5,3},{30,31},{31,30}} | collective-permute-start | bytes 786440 | tf_op jit(solution)/shard_map/ppermute | solution.py:435
  75.2 28.3 %collective-permute-start.12 = (f32[64,2304]{1,0:T(8,128)S(1)}, f32[64,2304]{1,0:T(8,128)S(1)}, u32[]{:S(2)}, u32[]{:S(2)}) collective-permute-start(f32[64,2304]{1,0:T(8,128)S(1)} %get-tuple-element.39), channel_id=1, source_target_pairs={{0,0},{25,2},{2,1},{27,4},{4,3},{29,6},{6,5},{23,8},{8,7},{17,10},... | collective-permute-start | bytes 1769480 | tf_op jit(solution)/shard_map/ppermute | solution.py:457
  77.1 26.4 %collective-permute-start.15 = (f32[64,2304]{1,0:T(8,128)S(1)}, f32[64,2304]{1,0:T(8,128)S(1)}, u32[]{:S(2)}, u32[]{:S(2)}) collective-permute-start(f32[64,2304]{1,0:T(8,128)S(1)} %get-tuple-element.42), channel_id=1, source_target_pairs={{0,1},{25,0},{2,3},{27,2},{4,5},{29,4},{6,7},{23,6},{8,9},{17,8},{... | collective-permute-start | bytes 1769480 | tf_op jit(solution)/shard_map/ppermute | solution.py:458
  77.2 13.2 %collective-permute-start.14 = (f32[64,768]{1,0:T(8,128)S(1)}, f32[64,768]{1,0:T(8,128)S(1)}, u32[]{:S(2)}, u32[]{:S(2)}) collective-permute-start(f32[64,768]{1,0:T(8,128)S(1)} %get-tuple-element.41), channel_id=1, source_target_pairs={{24,23},{1,26},{26,25},{3,28},{28,27},{5,30},{30,29},{31,31}} | collective-permute-start | bytes 589832 | tf_op jit(solution)/shard_map/ppermute | solution.py:457
  79.8 23.8 %collective-permute-start.13 = (f32[64,1024]{1,0:T(8,128)S(1)}, f32[64,1024]{1,0:T(8,128)S(1)}, u32[]{:S(2)}, u32[]{:S(2)}) collective-permute-start(f32[64,1024]{1,0:T(8,128)S(1)} %get-tuple-element.40), channel_id=1, source_target_pairs={{16,15},{9,18},{18,17},{11,20},{20,19},{13,22},{22,21},{7,24},{24,... | collective-permute-start | bytes 786440 | tf_op jit(solution)/shard_map/ppermute | solution.py:457
  81.7 21.9 %collective-permute-start.16 = (f32[64,1024]{1,0:T(8,128)S(1)}, f32[64,1024]{1,0:T(8,128)S(1)}, u32[]{:S(2)}, u32[]{:S(2)}) collective-permute-start(f32[64,1024]{1,0:T(8,128)S(1)} %get-tuple-element.43), channel_id=1, source_target_pairs={{16,17},{9,16},{18,19},{11,18},{20,21},{13,20},{22,23},{7,22},{24,... | collective-permute-start | bytes 786440 | tf_op jit(solution)/shard_map/ppermute | solution.py:458
  90.4 13.1 %collective-permute-start.17 = (f32[64,768]{1,0:T(8,128)S(1)}, f32[64,768]{1,0:T(8,128)S(1)}, u32[]{:S(2)}, u32[]{:S(2)}) collective-permute-start(f32[64,768]{1,0:T(8,128)S(1)} %get-tuple-element.44), channel_id=1, source_target_pairs={{24,25},{1,24},{26,27},{3,26},{28,29},{5,28},{30,31},{31,30}} | collective-permute-start | bytes 589832 | tf_op jit(solution)/shard_map/ppermute | solution.py:458
where the time goes:
time: 109 us
  waiting for transfers between devices  44.7 us (41%)
  starting transfers between devices  40.5 us (37%)
  Pallas kernels  21.4 us (20%)
  local copies, waits for them, and re-layouts  1.59 us (1%)
    ppermute x6, waiting for transfers between devices, swapped(): lax.ppermute(value, axes, swap_pairs(first_row, width, count, columns)[si...  17.4 us
    ppermute x6, starting transfers between devices, swapped(): lax.ppermute(value, axes, swap_pairs(first_row, width, count, columns)[si...  17.2 us
    ppermute x6, starting transfers between devices, per_device(): received[place] = lax.ppermute(chunks[place], axes, pairs)  12.9 us
    ppermute x3, waiting for transfers between devices, per_device(): on[place] = lax.ppermute(on[place], axes, on_pairs)  11 us
    pallas_call x1, Pallas kernels, per_device(): pl.pallas_call(functools.partial(middle_kernel, near_count), in_specs=in_...  10.7 us
    ppermute x6, waiting for transfers between devices, per_device(): received[place] = lax.ppermute(chunks[place], axes, pairs)  9.45 us
    ppermute x3, waiting for transfers between devices, per_device(): off[place] = lax.ppermute(off[place], axes, off_pairs)  6.81 us
    ppermute x3, starting transfers between devices, per_device(): off[place] = lax.ppermute(off[place], axes, off_pairs)  6.39 us
  transfers between devices with their start and end apart: 18, of which 9 were waited for; matrix products, arithmetic and copies ran while one was open for 0% of the time, Pallas kernels for 0%

commit v1 on v0

--- a/solution.py
+++ b/solution.py
@@ -404,7 +404,7 @@
         ],
         compiler_params=params,
         name="prepare",
-    )(factor_tiles.reshape(cycles, rows * tiles, width))
+    )(pltpu.with_memory_space_constraint(factor_tiles.reshape(cycles, rows * tiles, width), pltpu.HBM))
     received = list(chunks)
     for place, (offset, piece) in enumerate(order):
         if offset:

time: 109 us -> 108 us (level)
  local copies, waits for them, and re-layouts: 1.59 us -> 0 us
    unnamed x2 -> x0, local copies, waits for them, and re-layouts: 1.59 us -> none
where the time goes in v1:
time: 108 us
  waiting for transfers between devices  44.7 us (41%)
  starting transfers between devices  40.5 us (38%)
  Pallas kernels  22.2 us (21%)
    ppermute x6, waiting for transfers between devices, swapped(): lax.ppermute(value, axes, swap_pairs(first_row, width, count, columns)[si...  17.4 us
    ppermute x6, starting transfers between devices, swapped(): lax.ppermute(value, axes, swap_pairs(first_row, width, count, columns)[si...  17.2 us
    ppermute x6, starting transfers between devices, per_device(): received[place] = lax.ppermute(chunks[place], axes, pairs)  12.9 us
    ppermute x3, waiting for transfers between devices, per_device(): on[place] = lax.ppermute(on[place], axes, on_pairs)  11 us
    pallas_call x1, Pallas kernels, per_device(): pl.pallas_call(functools.partial(middle_kernel, near_count), in_specs=in_...  10.7 us
    ppermute x6, waiting for transfers between devices, per_device(): received[place] = lax.ppermute(chunks[place], axes, pairs)  9.45 us
    ppermute x3, waiting for transfers between devices, per_device(): off[place] = lax.ppermute(off[place], axes, off_pairs)  6.81 us
    ppermute x3, starting transfers between devices, per_device(): off[place] = lax.ppermute(off[place], axes, off_pairs)  6.39 us
  transfers between devices with their start and end apart: 18, of which 9 were waited for; matrix products, arithmetic and copies ran while one was open for 0% of the time, Pallas kernels for 0%

profile of v1, /device:TPU:22, one launch (start us, length us, event | category | flops | bytes accessed | tf_op | source)
XLA Modules:
  0.0 107.8 jit_solution(10504181805448156641)
XLA Ops:
  0.0 2.1 %prepare.1 = (f32[128,512]{1,0:T(8,128)S(1)}, f32[128,512]{1,0:T(8,128)S(1)}, f32[128,512]{1,0:T(8,128)S(1)}, f32[128,512]{1,0:T(8,128)S(1)}, f32[128,512]{1,0:T...) custom-call(f32[8,512,128]{2,1,0:T(8,128)} %bitcast.1), custom_call_target="tpu_custom_call" | custom-call | tf_op jit(solution)/shard_map/prepare/pallas_call | solution.py:396
  3.4 3.6 %collective-permute-start.1 = (f32[128,512]{1,0:T(8,128)S(1)}, f32[128,512]{1,0:T(8,128)S(1)}, u32[]{:S(2)}, u32[]{:S(2)}) collective-permute-start(f32[128,512]{1,0:T(8,128)S(1)} %get-tuple-element.26), channel_id=1, source_target_pairs={{0,24},{1,25},{2,26},{3,27},{4,28},{5,29},{6,30},{7,31},{8,16},{9,... | collective-permute-start | bytes 786440 | tf_op jit(solution)/shard_map/ppermute | solution.py:412
  8.3 2.7 %collective-permute-start.3 = (f32[128,512]{1,0:T(8,128)S(1)}, f32[128,512]{1,0:T(8,128)S(1)}, u32[]{:S(2)}, u32[]{:S(2)}) collective-permute-start(f32[128,512]{1,0:T(8,128)S(1)} %get-tuple-element.28), channel_id=1, source_target_pairs={{0,16},{1,17},{2,18},{3,19},{4,20},{5,21},{6,22},{7,23},{8,24},{9,... | collective-permute-start | bytes 786440 | tf_op jit(solution)/shard_map/ppermute | solution.py:412
  11.0 2.4 %collective-permute-start.4 = (f32[128,512]{1,0:T(8,128)S(1)}, f32[128,512]{1,0:T(8,128)S(1)}, u32[]{:S(2)}, u32[]{:S(2)}) collective-permute-start(f32[128,512]{1,0:T(8,128)S(1)} %get-tuple-element.29), channel_id=1, source_target_pairs={{1,9},{3,11},{5,13},{9,1},{11,3},{13,5},{15,7},{16,24},{18,26},{20... | collective-permute-start | bytes 786440 | tf_op jit(solution)/shard_map/ppermute | solution.py:412
  15.0 2.9 %collective-permute-done.1.refs_1_ = f32[128,512]{1,0:T(8,128)S(1)} collective-permute-done((f32[128,512]{1,0:T(8,128)S(1)}, f32[128,512]{1,0:T(8,128)S(1)}, u32[]{:S(2)}, u32[]{:S(2)}) %collective-permute-start.1) | collective-permute-done | bytes 262176 | tf_op jit(solution)/shard_map/ppermute | solution.py:412
  18.0 3.7 %collective-permute-done.2.refs_2_ = f32[128,512]{1,0:T(8,128)S(1)} collective-permute-done((f32[128,512]{1,0:T(8,128)S(1)}, f32[128,512]{1,0:T(8,128)S(1)}, u32[]{:S(2)}, u32[]{:S(2)}) %collective-permute-start.2) | collective-permute-done | bytes 262176 | tf_op jit(solution)/shard_map/ppermute | solution.py:412
  21.7 2.8 %collective-permute-done.3.refs_3_ = f32[128,512]{1,0:T(8,128)S(1)} collective-permute-done((f32[128,512]{1,0:T(8,128)S(1)}, f32[128,512]{1,0:T(8,128)S(1)}, u32[]{:S(2)}, u32[]{:S(2)}) %collective-permute-start.3) | collective-permute-done | bytes 262176 | tf_op jit(solution)/shard_map/ppermute | solution.py:412
  24.5 4.6 %first_round.1 = (f32[64,2048]{1,0:T(8,128)S(1)}, f32[64,1024]{1,0:T(8,128)S(1)}, f32[64,1024]{1,0:T(8,128)S(1)}, f32[64,1280]{1,0:T(8,128)S(1)}, f32[64,1536]{1,0:T(8,128)S(1)}, /*index=5*/f32[64,1280]{1,0:T(8,128)S(1)}) custom-call(f32[128,512]{1,0:T(8,128)S(1)} %collective-permute-done.refs_0_, f32[128,512]{1,0:T(8,128)S(1)} %collective-permute-done.1.refs_1_, ...), custom_call_target="tpu_custom_call" | custom-call | tf_op jit(solution)/shard_map/first_round/pallas_call | solution.py:423
  29.1 2.4 %collective-permute-start.7 = (f32[64,1024]{1,0:T(8,128)S(1)}, f32[64,1024]{1,0:T(8,128)S(1)}, u32[]{:S(2)}, u32[]{:S(2)}) collective-permute-start(f32[64,1024]{1,0:T(8,128)S(1)} %get-tuple-element.34.refs_7_), channel_id=1, source_target_pairs={{16,14},{9,15},{18,20},{11,13},{20,18},{13,11},{22,24},{7,1},{24,2... | collective-permute-start | bytes 786440 | tf_op jit(solution)/shard_map/ppermute | solution.py:435
  33.1 7.3 %collective-permute-start.10 = (f32[64,1536]{1,0:T(8,128)S(1)}, f32[64,1536]{1,0:T(8,128)S(1)}, u32[]{:S(2)}, u32[]{:S(2)}) collective-permute-start(f32[64,1536]{1,0:T(8,128)S(1)} %get-tuple-element.37.refs_10_), channel_id=1, source_target_pairs={{10,8},{19,17},{12,14},{21,15},{14,12},{15,21},{16,18},{9,11},{18,... | collective-permute-start | bytes 1179656 | tf_op jit(solution)/shard_map/ppermute | solution.py:435
  40.5 3.9 %collective-permute-start.11 = (f32[64,1280]{1,0:T(8,128)S(1)}, f32[64,1280]{1,0:T(8,128)S(1)}, u32[]{:S(2)}, u32[]{:S(2)}) collective-permute-start(f32[64,1280]{1,0:T(8,128)S(1)} %get-tuple-element.38.refs_11_), channel_id=1, source_target_pairs={{22,20},{7,13},{24,26},{1,3},{26,24},{3,1},{28,30},{5,31},{30,28},... | collective-permute-start | bytes 983048 | tf_op jit(solution)/shard_map/ppermute | solution.py:435
  44.4 2.8 %collective-permute-done.7.refs_1_ = f32[64,1024]{1,0:T(8,128)S(1)} collective-permute-done((f32[64,1024]{1,0:T(8,128)S(1)}, f32[64,1024]{1,0:T(8,128)S(1)}, u32[]{:S(2)}, u32[]{:S(2)}) %collective-permute-start.7) | collective-permute-done | bytes 262176 | tf_op jit(solution)/shard_map/ppermute | solution.py:435
  47.1 1.9 %collective-permute-start.8 = (f32[64,1024]{1,0:T(8,128)S(1)}, f32[64,1024]{1,0:T(8,128)S(1)}, u32[]{:S(2)}, u32[]{:S(2)}) collective-permute-start(f32[64,1024]{1,0:T(8,128)S(1)} %get-tuple-element.35.refs_8_), channel_id=1, source_target_pairs={{24,22},{1,7},{26,28},{3,5},{28,26},{5,3},{30,31},{31,30}} | collective-permute-start | bytes 786440 | tf_op jit(solution)/shard_map/ppermute | solution.py:435
  49.0 6.5 %collective-permute-done.8.refs_2_ = f32[64,1024]{1,0:T(8,128)S(1)} collective-permute-done((f32[64,1024]{1,0:T(8,128)S(1)}, f32[64,1024]{1,0:T(8,128)S(1)}, u32[]{:S(2)}, u32[]{:S(2)}) %collective-permute-start.8) | collective-permute-done | bytes 262176 | tf_op jit(solution)/shard_map/ppermute | solution.py:435
  57.3 6.4 %collective-permute-done.11.refs_5_ = f32[64,1280]{1,0:T(8,128)S(1)} collective-permute-done((f32[64,1280]{1,0:T(8,128)S(1)}, f32[64,1280]{1,0:T(8,128)S(1)}, u32[]{:S(2)}, u32[]{:S(2)}) %collective-permute-start.11) | collective-permute-done | bytes 327712 | tf_op jit(solution)/shard_map/ppermute | solution.py:435
  63.7 10.7 %middle_rounds.1 = (f32[64,2304]{1,0:T(8,128)S(1)}, f32[64,1024]{1,0:T(8,128)S(1)}, f32[64,768]{1,0:T(8,128)S(1)}, f32[64,2304]{1,0:T(8,128)S(1)}, f32[64,1024]{1,0:T(8,128)S(1)}, /*index=5*/f32[64,768]{1,0:T(8,128)S(1)}) custom-call(f32[64,2048]{1,0:T(8,128)S(1)} %collective-permute-done.6.refs_0_, f32[64,1024]{1,0:T(8,128)S(1)} %collective-permute-done.7.refs_1_, ...), custom_call_target="tpu_custom_call" | custom-call | tf_op jit(solution)/shard_map/middle_rounds/pallas_call | solution.py:445
  74.4 1.9 %collective-permute-start.12 = (f32[64,2304]{1,0:T(8,128)S(1)}, f32[64,2304]{1,0:T(8,128)S(1)}, u32[]{:S(2)}, u32[]{:S(2)}) collective-permute-start(f32[64,2304]{1,0:T(8,128)S(1)} %get-tuple-element.39), channel_id=1, source_target_pairs={{0,0},{25,2},{2,1},{27,4},{4,3},{29,6},{6,5},{23,8},{8,7},{17,10},... | collective-permute-start | bytes 1769480 | tf_op jit(solution)/shard_map/ppermute | solution.py:457
  76.4 2.5 %collective-permute-start.14 = (f32[64,768]{1,0:T(8,128)S(1)}, f32[64,768]{1,0:T(8,128)S(1)}, u32[]{:S(2)}, u32[]{:S(2)}) collective-permute-start(f32[64,768]{1,0:T(8,128)S(1)} %get-tuple-element.41), channel_id=1, source_target_pairs={{24,23},{1,26},{26,25},{3,28},{28,27},{5,30},{30,29},{31,31}} | collective-permute-start | bytes 589832 | tf_op jit(solution)/shard_map/ppermute | solution.py:457
  79.0 1.9 %collective-permute-start.13 = (f32[64,1024]{1,0:T(8,128)S(1)}, f32[64,1024]{1,0:T(8,128)S(1)}, u32[]{:S(2)}, u32[]{:S(2)}) collective-permute-start(f32[64,1024]{1,0:T(8,128)S(1)} %get-tuple-element.40), channel_id=1, source_target_pairs={{16,15},{9,18},{18,17},{11,20},{20,19},{13,22},{22,21},{7,24},{24,... | collective-permute-start | bytes 786440 | tf_op jit(solution)/shard_map/ppermute | solution.py:457
  80.9 1.9 %collective-permute-start.16 = (f32[64,1024]{1,0:T(8,128)S(1)}, f32[64,1024]{1,0:T(8,128)S(1)}, u32[]{:S(2)}, u32[]{:S(2)}) collective-permute-start(f32[64,1024]{1,0:T(8,128)S(1)} %get-tuple-element.43), channel_id=1, source_target_pairs={{16,17},{9,16},{18,19},{11,18},{20,21},{13,20},{22,23},{7,22},{24,... | collective-permute-start | bytes 786440 | tf_op jit(solution)/shard_map/ppermute | solution.py:458
  82.8 6.8 %collective-permute-done.14.refs_2_ = f32[64,768]{1,0:T(8,128)S(1)} collective-permute-done((f32[64,768]{1,0:T(8,128)S(1)}, f32[64,768]{1,0:T(8,128)S(1)}, u32[]{:S(2)}, u32[]{:S(2)}) %collective-permute-start.14) | collective-permute-done | bytes 196640 | tf_op jit(solution)/shard_map/ppermute | solution.py:457
  89.6 2.1 %collective-permute-start.17 = (f32[64,768]{1,0:T(8,128)S(1)}, f32[64,768]{1,0:T(8,128)S(1)}, u32[]{:S(2)}, u32[]{:S(2)}) collective-permute-start(f32[64,768]{1,0:T(8,128)S(1)} %get-tuple-element.44), channel_id=1, source_target_pairs={{24,25},{1,24},{26,27},{3,26},{28,29},{5,28},{30,31},{31,30}} | collective-permute-start | bytes 589832 | tf_op jit(solution)/shard_map/ppermute | solution.py:458
  91.7 11.0 %collective-permute-done.17.refs_5_ = f32[64,768]{1,0:T(8,128)S(1)} collective-permute-done((f32[64,768]{1,0:T(8,128)S(1)}, f32[64,768]{1,0:T(8,128)S(1)}, u32[]{:S(2)}, u32[]{:S(2)}) %collective-permute-start.17) | collective-permute-done | bytes 196640 | tf_op jit(solution)/shard_map/ppermute | solution.py:458
  102.8 4.9 %last_round.1 = f32[4096,128]{1,0:T(8,128)} custom-call(f32[64,2304]{1,0:T(8,128)S(1)} %collective-permute-done.12.refs_0_, f32[64,1024]{1,0:T(8,128)S(1)} %collective-permute-done.13.refs_1_, f32[64,768]{1,0:T(8,128)S(1)} %collective-permute-done.14.refs_2_, f32[64,2304]{1,0:T(8,128)S(1)} %collective-permute-done.15.refs_3_, ...), custom_call_target="tpu_custom_call" | custom-call | tf_op jit(solution)/shard_map/last_round/pallas_call | solution.py:459
  (16 shorter events, 7.7 us)
Async XLA Ops:
  2.1 11.4 %collective-permute-start = (f32[128,512]{1,0:T(8,128)S(1)}, f32[128,512]{1,0:T(8,128)S(1)}, u32[]{:S(2)}, u32[]{:S(2)}) collective-permute-start(f32[128,512]{1,0:T(8,128)S(1)} %get-tuple-element.25), channel_id=1, source_target_pairs={{0,24},{2,26},{4,28},{6,30},{7,31},{8,16},{10,18},{12,20},{14,22},... | collective-permute-start | bytes 786440 | tf_op jit(solution)/shard_map/ppermute | solution.py:412
  3.4 14.5 %collective-permute-start.1 = (f32[128,512]{1,0:T(8,128)S(1)}, f32[128,512]{1,0:T(8,128)S(1)}, u32[]{:S(2)}, u32[]{:S(2)}) collective-permute-start(f32[128,512]{1,0:T(8,128)S(1)} %get-tuple-element.26), channel_id=1, source_target_pairs={{0,24},{1,25},{2,26},{3,27},{4,28},{5,29},{6,30},{7,31},{8,16},{9,... | collective-permute-start | bytes 786440 | tf_op jit(solution)/shard_map/ppermute | solution.py:412
  7.0 14.6 %collective-permute-start.2 = (f32[128,512]{1,0:T(8,128)S(1)}, f32[128,512]{1,0:T(8,128)S(1)}, u32[]{:S(2)}, u32[]{:S(2)}) collective-permute-start(f32[128,512]{1,0:T(8,128)S(1)} %get-tuple-element.27), channel_id=1, source_target_pairs={{0,16},{2,18},{4,20},{6,22},{8,24},{10,26},{12,28},{14,30},{15,31}... | collective-permute-start | bytes 786440 | tf_op jit(solution)/shard_map/ppermute | solution.py:412
  8.3 16.2 %collective-permute-start.3 = (f32[128,512]{1,0:T(8,128)S(1)}, f32[128,512]{1,0:T(8,128)S(1)}, u32[]{:S(2)}, u32[]{:S(2)}) collective-permute-start(f32[128,512]{1,0:T(8,128)S(1)} %get-tuple-element.28), channel_id=1, source_target_pairs={{0,16},{1,17},{2,18},{3,19},{4,20},{5,21},{6,22},{7,23},{8,24},{9,... | collective-permute-start | bytes 786440 | tf_op jit(solution)/shard_map/ppermute | solution.py:412
  11.0 13.4 %collective-permute-start.4 = (f32[128,512]{1,0:T(8,128)S(1)}, f32[128,512]{1,0:T(8,128)S(1)}, u32[]{:S(2)}, u32[]{:S(2)}) collective-permute-start(f32[128,512]{1,0:T(8,128)S(1)} %get-tuple-element.29), channel_id=1, source_target_pairs={{1,9},{3,11},{5,13},{9,1},{11,3},{13,5},{15,7},{16,24},{18,26},{20... | collective-permute-start | bytes 786440 | tf_op jit(solution)/shard_map/ppermute | solution.py:412
  13.5 11.0 %collective-permute-start.5 = (f32[128,512]{1,0:T(8,128)S(1)}, f32[128,512]{1,0:T(8,128)S(1)}, u32[]{:S(2)}, u32[]{:S(2)}) collective-permute-start(f32[128,512]{1,0:T(8,128)S(1)} %get-tuple-element.30), channel_id=1, source_target_pairs={{0,8},{1,9},{2,10},{3,11},{4,12},{5,13},{6,14},{7,15},{8,0},{9,1},... | collective-permute-start | bytes 786440 | tf_op jit(solution)/shard_map/ppermute | solution.py:412
  29.1 18.0 %collective-permute-start.7 = (f32[64,1024]{1,0:T(8,128)S(1)}, f32[64,1024]{1,0:T(8,128)S(1)}, u32[]{:S(2)}, u32[]{:S(2)}) collective-permute-start(f32[64,1024]{1,0:T(8,128)S(1)} %get-tuple-element.34.refs_7_), channel_id=1, source_target_pairs={{16,14},{9,15},{18,20},{11,13},{20,18},{13,11},{22,24},{7,1},{24,2... | collective-permute-start | bytes 786440 | tf_op jit(solution)/shard_map/ppermute | solution.py:435
  31.4 32.3 %collective-permute-start.6 = (f32[64,2048]{1,0:T(8,128)S(1)}, f32[64,2048]{1,0:T(8,128)S(1)}, u32[]{:S(2)}, u32[]{:S(2)}) collective-permute-start(f32[64,2048]{1,0:T(8,128)S(1)} %get-tuple-element.33.refs_6_), channel_id=1, source_target_pairs={{0,25},{25,0},{2,4},{27,29},{4,2},{29,27},{6,8},{23,17},{8,6},{17,... | collective-permute-start | bytes 1572872 | tf_op jit(solution)/shard_map/ppermute | solution.py:435
  33.1 30.6 %collective-permute-start.10 = (f32[64,1536]{1,0:T(8,128)S(1)}, f32[64,1536]{1,0:T(8,128)S(1)}, u32[]{:S(2)}, u32[]{:S(2)}) collective-permute-start(f32[64,1536]{1,0:T(8,128)S(1)} %get-tuple-element.37.refs_10_), channel_id=1, source_target_pairs={{10,8},{19,17},{12,14},{21,15},{14,12},{15,21},{16,18},{9,11},{18,... | collective-permute-start | bytes 1179656 | tf_op jit(solution)/shard_map/ppermute | solution.py:435
  40.4 16.9 %collective-permute-start.9 = (f32[64,1280]{1,0:T(8,128)S(1)}, f32[64,1280]{1,0:T(8,128)S(1)}, u32[]{:S(2)}, u32[]{:S(2)}) collective-permute-start(f32[64,1280]{1,0:T(8,128)S(1)} %get-tuple-element.36.refs_9_), channel_id=1, source_target_pairs={{0,2},{25,27},{2,0},{27,25},{4,6},{29,23},{6,4},{23,29},{8,10},{17... | collective-permute-start | bytes 983048 | tf_op jit(solution)/shard_map/ppermute | solution.py:435
  40.5 23.3 %collective-permute-start.11 = (f32[64,1280]{1,0:T(8,128)S(1)}, f32[64,1280]{1,0:T(8,128)S(1)}, u32[]{:S(2)}, u32[]{:S(2)}) collective-permute-start(f32[64,1280]{1,0:T(8,128)S(1)} %get-tuple-element.38.refs_11_), channel_id=1, source_target_pairs={{22,20},{7,13},{24,26},{1,3},{26,24},{3,1},{28,30},{5,31},{30,28},... | collective-permute-start | bytes 983048 | tf_op jit(solution)/shard_map/ppermute | solution.py:435
  47.1 8.4 %collective-permute-start.8 = (f32[64,1024]{1,0:T(8,128)S(1)}, f32[64,1024]{1,0:T(8,128)S(1)}, u32[]{:S(2)}, u32[]{:S(2)}) collective-permute-start(f32[64,1024]{1,0:T(8,128)S(1)} %get-tuple-element.35.refs_8_), channel_id=1, source_target_pairs={{24,22},{1,7},{26,28},{3,5},{28,26},{5,3},{30,31},{31,30}} | collective-permute-start | bytes 786440 | tf_op jit(solution)/shard_map/ppermute | solution.py:435
  74.4 28.3 %collective-permute-start.12 = (f32[64,2304]{1,0:T(8,128)S(1)}, f32[64,2304]{1,0:T(8,128)S(1)}, u32[]{:S(2)}, u32[]{:S(2)}) collective-permute-start(f32[64,2304]{1,0:T(8,128)S(1)} %get-tuple-element.39), channel_id=1, source_target_pairs={{0,0},{25,2},{2,1},{27,4},{4,3},{29,6},{6,5},{23,8},{8,7},{17,10},... | collective-permute-start | bytes 1769480 | tf_op jit(solution)/shard_map/ppermute | solution.py:457
  76.3 26.4 %collective-permute-start.15 = (f32[64,2304]{1,0:T(8,128)S(1)}, f32[64,2304]{1,0:T(8,128)S(1)}, u32[]{:S(2)}, u32[]{:S(2)}) collective-permute-start(f32[64,2304]{1,0:T(8,128)S(1)} %get-tuple-element.42), channel_id=1, source_target_pairs={{0,1},{25,0},{2,3},{27,2},{4,5},{29,4},{6,7},{23,6},{8,9},{17,8},{... | collective-permute-start | bytes 1769480 | tf_op jit(solution)/shard_map/ppermute | solution.py:458
  76.4 13.2 %collective-permute-start.14 = (f32[64,768]{1,0:T(8,128)S(1)}, f32[64,768]{1,0:T(8,128)S(1)}, u32[]{:S(2)}, u32[]{:S(2)}) collective-permute-start(f32[64,768]{1,0:T(8,128)S(1)} %get-tuple-element.41), channel_id=1, source_target_pairs={{24,23},{1,26},{26,25},{3,28},{28,27},{5,30},{30,29},{31,31}} | collective-permute-start | bytes 589832 | tf_op jit(solution)/shard_map/ppermute | solution.py:457
  79.0 23.8 %collective-permute-start.13 = (f32[64,1024]{1,0:T(8,128)S(1)}, f32[64,1024]{1,0:T(8,128)S(1)}, u32[]{:S(2)}, u32[]{:S(2)}) collective-permute-start(f32[64,1024]{1,0:T(8,128)S(1)} %get-tuple-element.40), channel_id=1, source_target_pairs={{16,15},{9,18},{18,17},{11,20},{20,19},{13,22},{22,21},{7,24},{24,... | collective-permute-start | bytes 786440 | tf_op jit(solution)/shard_map/ppermute | solution.py:457
  80.9 21.9 %collective-permute-start.16 = (f32[64,1024]{1,0:T(8,128)S(1)}, f32[64,1024]{1,0:T(8,128)S(1)}, u32[]{:S(2)}, u32[]{:S(2)}) collective-permute-start(f32[64,1024]{1,0:T(8,128)S(1)} %get-tuple-element.43), channel_id=1, source_target_pairs={{16,17},{9,16},{18,19},{11,18},{20,21},{13,20},{22,23},{7,22},{24,... | collective-permute-start | bytes 786440 | tf_op jit(solution)/shard_map/ppermute | solution.py:458
  89.6 13.1 %collective-permute-start.17 = (f32[64,768]{1,0:T(8,128)S(1)}, f32[64,768]{1,0:T(8,128)S(1)}, u32[]{:S(2)}, u32[]{:S(2)}) collective-permute-start(f32[64,768]{1,0:T(8,128)S(1)} %get-tuple-element.44), channel_id=1, source_target_pairs={{24,25},{1,24},{26,27},{3,26},{28,29},{5,28},{30,31},{31,30}} | collective-permute-start | bytes 589832 | tf_op jit(solution)/shard_map/ppermute | solution.py:458

commit v2 on v1

--- a/solution.py
+++ b/solution.py
@@ -13,7 +13,6 @@
 LANES = 128
 SUBLANES = 8
 SPAN = 512
-DEPTH = 2048
 UNROLLED = 4096
 UNITS = 32
 NEAR_CUTS = (10, 22)
@@ -113,16 +112,23 @@
     order = split_ref.shape[0] // 3
     total = split_ref.shape[1]
 
-    def body(place, acc):
-        lanes = pl.ds(pl.multiple_of(place * DEPTH, DEPTH), DEPTH)
-        return acc + lax.dot_general(
+    def dot(lanes):
+        return lax.dot_general(
             split_ref[:, lanes],
             split_ref[: 2 * order, lanes],
             (((1,), (1,)), ((), ())),
             preferred_element_type=jnp.float32,
         )
 
-    acc = lax.fori_loop(0, total // DEPTH, body, jnp.zeros((3 * order, 2 * order), jnp.float32))
+    if total <= UNROLLED:
+        acc = dot(pl.ds(0, total))
+    else:
+        acc = lax.fori_loop(
+            0,
+            total // UNROLLED,
+            lambda place, acc: acc + dot(pl.ds(pl.multiple_of(place * UNROLLED, UNROLLED), UNROLLED)),
+            jnp.zeros((3 * order, 2 * order), jnp.float32),
+        )
     outer = acc[2 * order :, order:]
     inner = acc[:order, order:] + acc[order : 2 * order, :order] + acc[:order, :order]
     return acc[order : 2 * order, order:] + (inner + (outer + outer.T))

time: 108 us -> 110 us (1.019)
  Pallas kernels: 22.2 us -> 24.1 us
    pallas_call x1, Pallas kernels: 4.59 us -> 5.82 us  [per_device(): pl.pallas_call(functools.partial(first_kernel, order, near_count), in_spe...]
where the time goes in v2:
time: 110 us
  waiting for transfers between devices  44.7 us (41%)
  starting transfers between devices  40.5 us (37%)
  Pallas kernels  24.1 us (22%)
    ppermute x6, starting transfers between devices, swapped(): lax.ppermute(value, axes, swap_pairs(first_row, width, count, columns)[si...  17.4 us
    ppermute x6, waiting for transfers between devices, swapped(): lax.ppermute(value, axes, swap_pairs(first_row, width, count, columns)[si...  17.2 us
    ppermute x6, starting transfers between devices, per_device(): received[place] = lax.ppermute(chunks[place], axes, pairs)  12.9 us
    ppermute x3, waiting for transfers between devices, per_device(): on[place] = lax.ppermute(on[place], axes, on_pairs)  11.2 us
    pallas_call x1, Pallas kernels, per_device(): pl.pallas_call(functools.partial(middle_kernel, near_count), in_specs=in_...  11 us
    ppermute x6, waiting for transfers between devices, per_device(): received[place] = lax.ppermute(chunks[place], axes, pairs)  9.45 us
    ppermute x3, waiting for transfers between devices, per_device(): off[place] = lax.ppermute(off[place], axes, off_pairs)  6.8 us
    ppermute x3, starting transfers between devices, per_device(): off[place] = lax.ppermute(off[place], axes, off_pairs)  6.39 us
  transfers between devices with their start and end apart: 18, of which 9 were waited for; matrix products, arithmetic and copies ran while one was open for 0% of the time, Pallas kernels for 0%

profile of v2, /device:TPU:22, one launch (start us, length us, event | category | flops | bytes accessed | tf_op | source)
XLA Modules:
  0.0 109.7 jit_solution(4316053008097054717)
XLA Ops:
  0.0 2.1 %prepare.1 = (f32[128,512]{1,0:T(8,128)S(1)}, f32[128,512]{1,0:T(8,128)S(1)}, f32[128,512]{1,0:T(8,128)S(1)}, f32[128,512]{1,0:T(8,128)S(1)}, f32[128,512]{1,0:T...) custom-call(f32[8,512,128]{2,1,0:T(8,128)} %bitcast.1), custom_call_target="tpu_custom_call" | custom-call | tf_op jit(solution)/shard_map/prepare/pallas_call | solution.py:402
  3.4 3.6 %collective-permute-start.1 = (f32[128,512]{1,0:T(8,128)S(1)}, f32[128,512]{1,0:T(8,128)S(1)}, u32[]{:S(2)}, u32[]{:S(2)}) collective-permute-start(f32[128,512]{1,0:T(8,128)S(1)} %get-tuple-element.26), channel_id=1, source_target_pairs={{0,24},{1,25},{2,26},{3,27},{4,28},{5,29},{6,30},{7,31},{8,16},{9,... | collective-permute-start | bytes 786440 | tf_op jit(solution)/shard_map/ppermute | solution.py:418
  8.3 2.7 %collective-permute-start.3 = (f32[128,512]{1,0:T(8,128)S(1)}, f32[128,512]{1,0:T(8,128)S(1)}, u32[]{:S(2)}, u32[]{:S(2)}) collective-permute-start(f32[128,512]{1,0:T(8,128)S(1)} %get-tuple-element.28), channel_id=1, source_target_pairs={{0,16},{1,17},{2,18},{3,19},{4,20},{5,21},{6,22},{7,23},{8,24},{9,... | collective-permute-start | bytes 786440 | tf_op jit(solution)/shard_map/ppermute | solution.py:418
  11.0 2.4 %collective-permute-start.4 = (f32[128,512]{1,0:T(8,128)S(1)}, f32[128,512]{1,0:T(8,128)S(1)}, u32[]{:S(2)}, u32[]{:S(2)}) collective-permute-start(f32[128,512]{1,0:T(8,128)S(1)} %get-tuple-element.29), channel_id=1, source_target_pairs={{1,9},{3,11},{5,13},{9,1},{11,3},{13,5},{15,7},{16,24},{18,26},{20... | collective-permute-start | bytes 786440 | tf_op jit(solution)/shard_map/ppermute | solution.py:418
  15.0 2.9 %collective-permute-done.1.refs_1_ = f32[128,512]{1,0:T(8,128)S(1)} collective-permute-done((f32[128,512]{1,0:T(8,128)S(1)}, f32[128,512]{1,0:T(8,128)S(1)}, u32[]{:S(2)}, u32[]{:S(2)}) %collective-permute-start.1) | collective-permute-done | bytes 262176 | tf_op jit(solution)/shard_map/ppermute | solution.py:418
  18.0 3.7 %collective-permute-done.2.refs_2_ = f32[128,512]{1,0:T(8,128)S(1)} collective-permute-done((f32[128,512]{1,0:T(8,128)S(1)}, f32[128,512]{1,0:T(8,128)S(1)}, u32[]{:S(2)}, u32[]{:S(2)}) %collective-permute-start.2) | collective-permute-done | bytes 262176 | tf_op jit(solution)/shard_map/ppermute | solution.py:418
  21.7 2.8 %collective-permute-done.3.refs_3_ = f32[128,512]{1,0:T(8,128)S(1)} collective-permute-done((f32[128,512]{1,0:T(8,128)S(1)}, f32[128,512]{1,0:T(8,128)S(1)}, u32[]{:S(2)}, u32[]{:S(2)}) %collective-permute-start.3) | collective-permute-done | bytes 262176 | tf_op jit(solution)/shard_map/ppermute | solution.py:418
  24.5 5.8 %first_round.1 = (f32[64,2048]{1,0:T(8,128)S(1)}, f32[64,1024]{1,0:T(8,128)S(1)}, f32[64,1024]{1,0:T(8,128)S(1)}, f32[64,1280]{1,0:T(8,128)S(1)}, f32[64,1536]{1,0:T(8,128)S(1)}, /*index=5*/f32[64,1280]{1,0:T(8,128)S(1)}) custom-call(f32[128,512]{1,0:T(8,128)S(1)} %collective-permute-done.refs_0_, f32[128,512]{1,0:T(8,128)S(1)} %collective-permute-done.1.refs_1_, ...), custom_call_target="tpu_custom_call" | custom-call | tf_op jit(solution)/shard_map/first_round/pallas_call | solution.py:429
  30.3 2.4 %collective-permute-start.7 = (f32[64,1024]{1,0:T(8,128)S(1)}, f32[64,1024]{1,0:T(8,128)S(1)}, u32[]{:S(2)}, u32[]{:S(2)}) collective-permute-start(f32[64,1024]{1,0:T(8,128)S(1)} %get-tuple-element.34.refs_7_), channel_id=1, source_target_pairs={{16,14},{9,15},{18,20},{11,13},{20,18},{13,11},{22,24},{7,1},{24,2... | collective-permute-start | bytes 786440 | tf_op jit(solution)/shard_map/ppermute | solution.py:441
  34.3 7.3 %collective-permute-start.10 = (f32[64,1536]{1,0:T(8,128)S(1)}, f32[64,1536]{1,0:T(8,128)S(1)}, u32[]{:S(2)}, u32[]{:S(2)}) collective-permute-start(f32[64,1536]{1,0:T(8,128)S(1)} %get-tuple-element.37.refs_10_), channel_id=1, source_target_pairs={{10,8},{19,17},{12,14},{21,15},{14,12},{15,21},{16,18},{9,11},{18,... | collective-permute-start | bytes 1179656 | tf_op jit(solution)/shard_map/ppermute | solution.py:441
  41.7 3.9 %collective-permute-start.11 = (f32[64,1280]{1,0:T(8,128)S(1)}, f32[64,1280]{1,0:T(8,128)S(1)}, u32[]{:S(2)}, u32[]{:S(2)}) collective-permute-start(f32[64,1280]{1,0:T(8,128)S(1)} %get-tuple-element.38.refs_11_), channel_id=1, source_target_pairs={{22,20},{7,13},{24,26},{1,3},{26,24},{3,1},{28,30},{5,31},{30,28},... | collective-permute-start | bytes 983048 | tf_op jit(solution)/shard_map/ppermute | solution.py:441
  45.6 2.8 %collective-permute-done.7.refs_1_ = f32[64,1024]{1,0:T(8,128)S(1)} collective-permute-done((f32[64,1024]{1,0:T(8,128)S(1)}, f32[64,1024]{1,0:T(8,128)S(1)}, u32[]{:S(2)}, u32[]{:S(2)}) %collective-permute-start.7) | collective-permute-done | bytes 262176 | tf_op jit(solution)/shard_map/ppermute | solution.py:441
  48.4 2.1 %collective-permute-start.8 = (f32[64,1024]{1,0:T(8,128)S(1)}, f32[64,1024]{1,0:T(8,128)S(1)}, u32[]{:S(2)}, u32[]{:S(2)}) collective-permute-start(f32[64,1024]{1,0:T(8,128)S(1)} %get-tuple-element.35.refs_8_), channel_id=1, source_target_pairs={{24,22},{1,7},{26,28},{3,5},{28,26},{5,3},{30,31},{31,30}} | collective-permute-start | bytes 786440 | tf_op jit(solution)/shard_map/ppermute | solution.py:441
  50.5 6.3 %collective-permute-done.8.refs_2_ = f32[64,1024]{1,0:T(8,128)S(1)} collective-permute-done((f32[64,1024]{1,0:T(8,128)S(1)}, f32[64,1024]{1,0:T(8,128)S(1)}, u32[]{:S(2)}, u32[]{:S(2)}) %collective-permute-start.8) | collective-permute-done | bytes 262176 | tf_op jit(solution)/shard_map/ppermute | solution.py:441
  58.5 6.4 %collective-permute-done.11.refs_5_ = f32[64,1280]{1,0:T(8,128)S(1)} collective-permute-done((f32[64,1280]{1,0:T(8,128)S(1)}, f32[64,1280]{1,0:T(8,128)S(1)}, u32[]{:S(2)}, u32[]{:S(2)}) %collective-permute-start.11) | collective-permute-done | bytes 327712 | tf_op jit(solution)/shard_map/ppermute | solution.py:441
  65.0 11.0 %middle_rounds.1 = (f32[64,2304]{1,0:T(8,128)S(1)}, f32[64,1024]{1,0:T(8,128)S(1)}, f32[64,768]{1,0:T(8,128)S(1)}, f32[64,2304]{1,0:T(8,128)S(1)}, f32[64,1024]{1,0:T(8,128)S(1)}, /*index=5*/f32[64,768]{1,0:T(8,128)S(1)}) custom-call(f32[64,2048]{1,0:T(8,128)S(1)} %collective-permute-done.6.refs_0_, f32[64,1024]{1,0:T(8,128)S(1)} %collective-permute-done.7.refs_1_, ...), custom_call_target="tpu_custom_call" | custom-call | tf_op jit(solution)/shard_map/middle_rounds/pallas_call | solution.py:451
  75.9 1.9 %collective-permute-start.12 = (f32[64,2304]{1,0:T(8,128)S(1)}, f32[64,2304]{1,0:T(8,128)S(1)}, u32[]{:S(2)}, u32[]{:S(2)}) collective-permute-start(f32[64,2304]{1,0:T(8,128)S(1)} %get-tuple-element.39), channel_id=1, source_target_pairs={{0,0},{25,2},{2,1},{27,4},{4,3},{29,6},{6,5},{23,8},{8,7},{17,10},... | collective-permute-start | bytes 1769480 | tf_op jit(solution)/shard_map/ppermute | solution.py:463
  77.9 2.6 %collective-permute-start.14 = (f32[64,768]{1,0:T(8,128)S(1)}, f32[64,768]{1,0:T(8,128)S(1)}, u32[]{:S(2)}, u32[]{:S(2)}) collective-permute-start(f32[64,768]{1,0:T(8,128)S(1)} %get-tuple-element.41), channel_id=1, source_target_pairs={{24,23},{1,26},{26,25},{3,28},{28,27},{5,30},{30,29},{31,31}} | collective-permute-start | bytes 589832 | tf_op jit(solution)/shard_map/ppermute | solution.py:463
  80.5 1.9 %collective-permute-start.13 = (f32[64,1024]{1,0:T(8,128)S(1)}, f32[64,1024]{1,0:T(8,128)S(1)}, u32[]{:S(2)}, u32[]{:S(2)}) collective-permute-start(f32[64,1024]{1,0:T(8,128)S(1)} %get-tuple-element.40), channel_id=1, source_target_pairs={{16,15},{9,18},{18,17},{11,20},{20,19},{13,22},{22,21},{7,24},{24,... | collective-permute-start | bytes 786440 | tf_op jit(solution)/shard_map/ppermute | solution.py:463
  82.4 1.9 %collective-permute-start.16 = (f32[64,1024]{1,0:T(8,128)S(1)}, f32[64,1024]{1,0:T(8,128)S(1)}, u32[]{:S(2)}, u32[]{:S(2)}) collective-permute-start(f32[64,1024]{1,0:T(8,128)S(1)} %get-tuple-element.43), channel_id=1, source_target_pairs={{16,17},{9,16},{18,19},{11,18},{20,21},{13,20},{22,23},{7,22},{24,... | collective-permute-start | bytes 786440 | tf_op jit(solution)/shard_map/ppermute | solution.py:464
  84.3 6.8 %collective-permute-done.14.refs_2_ = f32[64,768]{1,0:T(8,128)S(1)} collective-permute-done((f32[64,768]{1,0:T(8,128)S(1)}, f32[64,768]{1,0:T(8,128)S(1)}, u32[]{:S(2)}, u32[]{:S(2)}) %collective-permute-start.14) | collective-permute-done | bytes 196640 | tf_op jit(solution)/shard_map/ppermute | solution.py:463
  91.1 1.9 %collective-permute-start.17 = (f32[64,768]{1,0:T(8,128)S(1)}, f32[64,768]{1,0:T(8,128)S(1)}, u32[]{:S(2)}, u32[]{:S(2)}) collective-permute-start(f32[64,768]{1,0:T(8,128)S(1)} %get-tuple-element.44), channel_id=1, source_target_pairs={{24,25},{1,24},{26,27},{3,26},{28,29},{5,28},{30,31},{31,30}} | collective-permute-start | bytes 589832 | tf_op jit(solution)/shard_map/ppermute | solution.py:464
  93.0 11.2 %collective-permute-done.17.refs_5_ = f32[64,768]{1,0:T(8,128)S(1)} collective-permute-done((f32[64,768]{1,0:T(8,128)S(1)}, f32[64,768]{1,0:T(8,128)S(1)}, u32[]{:S(2)}, u32[]{:S(2)}) %collective-permute-start.17) | collective-permute-done | bytes 196640 | tf_op jit(solution)/shard_map/ppermute | solution.py:464
  104.3 5.3 %last_round.1 = f32[4096,128]{1,0:T(8,128)} custom-call(f32[64,2304]{1,0:T(8,128)S(1)} %collective-permute-done.12.refs_0_, f32[64,1024]{1,0:T(8,128)S(1)} %collective-permute-done.13.refs_1_, f32[64,768]{1,0:T(8,128)S(1)} %collective-permute-done.14.refs_2_, f32[64,2304]{1,0:T(8,128)S(1)} %collective-permute-done.15.refs_3_, ...), custom_call_target="tpu_custom_call" | custom-call | tf_op jit(solution)/shard_map/last_round/pallas_call | solution.py:465
  (16 shorter events, 7.7 us)
Async XLA Ops:
  2.1 11.4 %collective-permute-start = (f32[128,512]{1,0:T(8,128)S(1)}, f32[128,512]{1,0:T(8,128)S(1)}, u32[]{:S(2)}, u32[]{:S(2)}) collective-permute-start(f32[128,512]{1,0:T(8,128)S(1)} %get-tuple-element.25), channel_id=1, source_target_pairs={{0,24},{2,26},{4,28},{6,30},{7,31},{8,16},{10,18},{12,20},{14,22},... | collective-permute-start | bytes 786440 | tf_op jit(solution)/shard_map/ppermute | solution.py:418
  3.4 14.5 %collective-permute-start.1 = (f32[128,512]{1,0:T(8,128)S(1)}, f32[128,512]{1,0:T(8,128)S(1)}, u32[]{:S(2)}, u32[]{:S(2)}) collective-permute-start(f32[128,512]{1,0:T(8,128)S(1)} %get-tuple-element.26), channel_id=1, source_target_pairs={{0,24},{1,25},{2,26},{3,27},{4,28},{5,29},{6,30},{7,31},{8,16},{9,... | collective-permute-start | bytes 786440 | tf_op jit(solution)/shard_map/ppermute | solution.py:418
  7.0 14.6 %collective-permute-start.2 = (f32[128,512]{1,0:T(8,128)S(1)}, f32[128,512]{1,0:T(8,128)S(1)}, u32[]{:S(2)}, u32[]{:S(2)}) collective-permute-start(f32[128,512]{1,0:T(8,128)S(1)} %get-tuple-element.27), channel_id=1, source_target_pairs={{0,16},{2,18},{4,20},{6,22},{8,24},{10,26},{12,28},{14,30},{15,31}... | collective-permute-start | bytes 786440 | tf_op jit(solution)/shard_map/ppermute | solution.py:418
  8.3 16.2 %collective-permute-start.3 = (f32[128,512]{1,0:T(8,128)S(1)}, f32[128,512]{1,0:T(8,128)S(1)}, u32[]{:S(2)}, u32[]{:S(2)}) collective-permute-start(f32[128,512]{1,0:T(8,128)S(1)} %get-tuple-element.28), channel_id=1, source_target_pairs={{0,16},{1,17},{2,18},{3,19},{4,20},{5,21},{6,22},{7,23},{8,24},{9,... | collective-permute-start | bytes 786440 | tf_op jit(solution)/shard_map/ppermute | solution.py:418
  11.0 13.4 %collective-permute-start.4 = (f32[128,512]{1,0:T(8,128)S(1)}, f32[128,512]{1,0:T(8,128)S(1)}, u32[]{:S(2)}, u32[]{:S(2)}) collective-permute-start(f32[128,512]{1,0:T(8,128)S(1)} %get-tuple-element.29), channel_id=1, source_target_pairs={{1,9},{3,11},{5,13},{9,1},{11,3},{13,5},{15,7},{16,24},{18,26},{20... | collective-permute-start | bytes 786440 | tf_op jit(solution)/shard_map/ppermute | solution.py:418
  13.5 11.0 %collective-permute-start.5 = (f32[128,512]{1,0:T(8,128)S(1)}, f32[128,512]{1,0:T(8,128)S(1)}, u32[]{:S(2)}, u32[]{:S(2)}) collective-permute-start(f32[128,512]{1,0:T(8,128)S(1)} %get-tuple-element.30), channel_id=1, source_target_pairs={{0,8},{1,9},{2,10},{3,11},{4,12},{5,13},{6,14},{7,15},{8,0},{9,1},... | collective-permute-start | bytes 786440 | tf_op jit(solution)/shard_map/ppermute | solution.py:418
  30.3 18.0 %collective-permute-start.7 = (f32[64,1024]{1,0:T(8,128)S(1)}, f32[64,1024]{1,0:T(8,128)S(1)}, u32[]{:S(2)}, u32[]{:S(2)}) collective-permute-start(f32[64,1024]{1,0:T(8,128)S(1)} %get-tuple-element.34.refs_7_), channel_id=1, source_target_pairs={{16,14},{9,15},{18,20},{11,13},{20,18},{13,11},{22,24},{7,1},{24,2... | collective-permute-start | bytes 786440 | tf_op jit(solution)/shard_map/ppermute | solution.py:441
  32.7 32.3 %collective-permute-start.6 = (f32[64,2048]{1,0:T(8,128)S(1)}, f32[64,2048]{1,0:T(8,128)S(1)}, u32[]{:S(2)}, u32[]{:S(2)}) collective-permute-start(f32[64,2048]{1,0:T(8,128)S(1)} %get-tuple-element.33.refs_6_), channel_id=1, source_target_pairs={{0,25},{25,0},{2,4},{27,29},{4,2},{29,27},{6,8},{23,17},{8,6},{17,... | collective-permute-start | bytes 1572872 | tf_op jit(solution)/shard_map/ppermute | solution.py:441
  34.3 30.6 %collective-permute-start.10 = (f32[64,1536]{1,0:T(8,128)S(1)}, f32[64,1536]{1,0:T(8,128)S(1)}, u32[]{:S(2)}, u32[]{:S(2)}) collective-permute-start(f32[64,1536]{1,0:T(8,128)S(1)} %get-tuple-element.37.refs_10_), channel_id=1, source_target_pairs={{10,8},{19,17},{12,14},{21,15},{14,12},{15,21},{16,18},{9,11},{18,... | collective-permute-start | bytes 1179656 | tf_op jit(solution)/shard_map/ppermute | solution.py:441
  41.6 16.9 %collective-permute-start.9 = (f32[64,1280]{1,0:T(8,128)S(1)}, f32[64,1280]{1,0:T(8,128)S(1)}, u32[]{:S(2)}, u32[]{:S(2)}) collective-permute-start(f32[64,1280]{1,0:T(8,128)S(1)} %get-tuple-element.36.refs_9_), channel_id=1, source_target_pairs={{0,2},{25,27},{2,0},{27,25},{4,6},{29,23},{6,4},{23,29},{8,10},{17... | collective-permute-start | bytes 983048 | tf_op jit(solution)/shard_map/ppermute | solution.py:441
  41.7 23.3 %collective-permute-start.11 = (f32[64,1280]{1,0:T(8,128)S(1)}, f32[64,1280]{1,0:T(8,128)S(1)}, u32[]{:S(2)}, u32[]{:S(2)}) collective-permute-start(f32[64,1280]{1,0:T(8,128)S(1)} %get-tuple-element.38.refs_11_), channel_id=1, source_target_pairs={{22,20},{7,13},{24,26},{1,3},{26,24},{3,1},{28,30},{5,31},{30,28},... | collective-permute-start | bytes 983048 | tf_op jit(solution)/shard_map/ppermute | solution.py:441
  48.4 8.4 %collective-permute-start.8 = (f32[64,1024]{1,0:T(8,128)S(1)}, f32[64,1024]{1,0:T(8,128)S(1)}, u32[]{:S(2)}, u32[]{:S(2)}) collective-permute-start(f32[64,1024]{1,0:T(8,128)S(1)} %get-tuple-element.35.refs_8_), channel_id=1, source_target_pairs={{24,22},{1,7},{26,28},{3,5},{28,26},{5,3},{30,31},{31,30}} | collective-permute-start | bytes 786440 | tf_op jit(solution)/shard_map/ppermute | solution.py:441
  75.9 28.3 %collective-permute-start.12 = (f32[64,2304]{1,0:T(8,128)S(1)}, f32[64,2304]{1,0:T(8,128)S(1)}, u32[]{:S(2)}, u32[]{:S(2)}) collective-permute-start(f32[64,2304]{1,0:T(8,128)S(1)} %get-tuple-element.39), channel_id=1, source_target_pairs={{0,0},{25,2},{2,1},{27,4},{4,3},{29,6},{6,5},{23,8},{8,7},{17,10},... | collective-permute-start | bytes 1769480 | tf_op jit(solution)/shard_map/ppermute | solution.py:463
  77.8 26.4 %collective-permute-start.15 = (f32[64,2304]{1,0:T(8,128)S(1)}, f32[64,2304]{1,0:T(8,128)S(1)}, u32[]{:S(2)}, u32[]{:S(2)}) collective-permute-start(f32[64,2304]{1,0:T(8,128)S(1)} %get-tuple-element.42), channel_id=1, source_target_pairs={{0,1},{25,0},{2,3},{27,2},{4,5},{29,4},{6,7},{23,6},{8,9},{17,8},{... | collective-permute-start | bytes 1769480 | tf_op jit(solution)/shard_map/ppermute | solution.py:464
  77.9 13.2 %collective-permute-start.14 = (f32[64,768]{1,0:T(8,128)S(1)}, f32[64,768]{1,0:T(8,128)S(1)}, u32[]{:S(2)}, u32[]{:S(2)}) collective-permute-start(f32[64,768]{1,0:T(8,128)S(1)} %get-tuple-element.41), channel_id=1, source_target_pairs={{24,23},{1,26},{26,25},{3,28},{28,27},{5,30},{30,29},{31,31}} | collective-permute-start | bytes 589832 | tf_op jit(solution)/shard_map/ppermute | solution.py:463
  80.5 23.8 %collective-permute-start.13 = (f32[64,1024]{1,0:T(8,128)S(1)}, f32[64,1024]{1,0:T(8,128)S(1)}, u32[]{:S(2)}, u32[]{:S(2)}) collective-permute-start(f32[64,1024]{1,0:T(8,128)S(1)} %get-tuple-element.40), channel_id=1, source_target_pairs={{16,15},{9,18},{18,17},{11,20},{20,19},{13,22},{22,21},{7,24},{24,... | collective-permute-start | bytes 786440 | tf_op jit(solution)/shard_map/ppermute | solution.py:463
  82.4 21.9 %collective-permute-start.16 = (f32[64,1024]{1,0:T(8,128)S(1)}, f32[64,1024]{1,0:T(8,128)S(1)}, u32[]{:S(2)}, u32[]{:S(2)}) collective-permute-start(f32[64,1024]{1,0:T(8,128)S(1)} %get-tuple-element.43), channel_id=1, source_target_pairs={{16,17},{9,16},{18,19},{11,18},{20,21},{13,20},{22,23},{7,22},{24,... | collective-permute-start | bytes 786440 | tf_op jit(solution)/shard_map/ppermute | solution.py:464
  91.1 13.1 %collective-permute-start.17 = (f32[64,768]{1,0:T(8,128)S(1)}, f32[64,768]{1,0:T(8,128)S(1)}, u32[]{:S(2)}, u32[]{:S(2)}) collective-permute-start(f32[64,768]{1,0:T(8,128)S(1)} %get-tuple-element.44), channel_id=1, source_target_pairs={{24,25},{1,24},{26,27},{3,26},{28,29},{5,28},{30,31},{31,30}} | collective-permute-start | bytes 589832 | tf_op jit(solution)/shard_map/ppermute | solution.py:464

commit v3 on v1

--- a/solution.py
+++ b/solution.py
@@ -13,7 +13,7 @@
 LANES = 128
 SUBLANES = 8
 SPAN = 512
-DEPTH = 2048
+DEPTH = 1024
 UNROLLED = 4096
 UNITS = 32
 NEAR_CUTS = (10, 22)

time: 108 us -> 110 us (1.019)
  Pallas kernels: 22.2 us -> 24.4 us
    pallas_call x1, Pallas kernels: 10.7 us -> 12 us  [per_device(): pl.pallas_call(functools.partial(middle_kernel, near_count), in_specs=in_...]
where the time goes in v3:
time: 110 us
  waiting for transfers between devices  44.9 us (41%)
  starting transfers between devices  40.3 us (37%)
  Pallas kernels  24.4 us (22%)
    ppermute x6, waiting for transfers between devices, swapped(): lax.ppermute(value, axes, swap_pairs(first_row, width, count, columns)[si...  17.4 us
    ppermute x6, starting transfers between devices, swapped(): lax.ppermute(value, axes, swap_pairs(first_row, width, count, columns)[si...  17.2 us
    ppermute x6, starting transfers between devices, per_device(): received[place] = lax.ppermute(chunks[place], axes, pairs)  12.9 us
    pallas_call x1, Pallas kernels, per_device(): pl.pallas_call(functools.partial(middle_kernel, near_count), in_specs=in_...  12 us
    ppermute x3, waiting for transfers between devices, per_device(): on[place] = lax.ppermute(on[place], axes, on_pairs)  11.2 us
    ppermute x6, waiting for transfers between devices, per_device(): received[place] = lax.ppermute(chunks[place], axes, pairs)  9.45 us
    ppermute x3, waiting for transfers between devices, per_device(): off[place] = lax.ppermute(off[place], axes, off_pairs)  6.82 us
    ppermute x3, starting transfers between devices, per_device(): off[place] = lax.ppermute(off[place], axes, off_pairs)  6.38 us
  transfers between devices with their start and end apart: 18, of which 9 were waited for; matrix products, arithmetic and copies ran while one was open for 0% of the time, Pallas kernels for 0%

profile of v3, /device:TPU:22, one launch (start us, length us, event | category | flops | bytes accessed | tf_op | source)
XLA Modules:
  0.0 109.8 jit_solution(15975279354803361685)
XLA Ops:
  0.0 2.1 %prepare.1 = (f32[128,512]{1,0:T(8,128)S(1)}, f32[128,512]{1,0:T(8,128)S(1)}, f32[128,512]{1,0:T(8,128)S(1)}, f32[128,512]{1,0:T(8,128)S(1)}, f32[128,512]{1,0:T...) custom-call(f32[8,512,128]{2,1,0:T(8,128)} %bitcast.1), custom_call_target="tpu_custom_call" | custom-call | tf_op jit(solution)/shard_map/prepare/pallas_call | solution.py:396
  3.4 3.6 %collective-permute-start.1 = (f32[128,512]{1,0:T(8,128)S(1)}, f32[128,512]{1,0:T(8,128)S(1)}, u32[]{:S(2)}, u32[]{:S(2)}) collective-permute-start(f32[128,512]{1,0:T(8,128)S(1)} %get-tuple-element.26), channel_id=1, source_target_pairs={{0,24},{1,25},{2,26},{3,27},{4,28},{5,29},{6,30},{7,31},{8,16},{9,... | collective-permute-start | bytes 786440 | tf_op jit(solution)/shard_map/ppermute | solution.py:412
  8.3 2.7 %collective-permute-start.3 = (f32[128,512]{1,0:T(8,128)S(1)}, f32[128,512]{1,0:T(8,128)S(1)}, u32[]{:S(2)}, u32[]{:S(2)}) collective-permute-start(f32[128,512]{1,0:T(8,128)S(1)} %get-tuple-element.28), channel_id=1, source_target_pairs={{0,16},{1,17},{2,18},{3,19},{4,20},{5,21},{6,22},{7,23},{8,24},{9,... | collective-permute-start | bytes 786440 | tf_op jit(solution)/shard_map/ppermute | solution.py:412
  11.0 2.4 %collective-permute-start.4 = (f32[128,512]{1,0:T(8,128)S(1)}, f32[128,512]{1,0:T(8,128)S(1)}, u32[]{:S(2)}, u32[]{:S(2)}) collective-permute-start(f32[128,512]{1,0:T(8,128)S(1)} %get-tuple-element.29), channel_id=1, source_target_pairs={{1,9},{3,11},{5,13},{9,1},{11,3},{13,5},{15,7},{16,24},{18,26},{20... | collective-permute-start | bytes 786440 | tf_op jit(solution)/shard_map/ppermute | solution.py:412
  15.0 2.9 %collective-permute-done.1.refs_1_ = f32[128,512]{1,0:T(8,128)S(1)} collective-permute-done((f32[128,512]{1,0:T(8,128)S(1)}, f32[128,512]{1,0:T(8,128)S(1)}, u32[]{:S(2)}, u32[]{:S(2)}) %collective-permute-start.1) | collective-permute-done | bytes 262176 | tf_op jit(solution)/shard_map/ppermute | solution.py:412
  18.0 3.7 %collective-permute-done.2.refs_2_ = f32[128,512]{1,0:T(8,128)S(1)} collective-permute-done((f32[128,512]{1,0:T(8,128)S(1)}, f32[128,512]{1,0:T(8,128)S(1)}, u32[]{:S(2)}, u32[]{:S(2)}) %collective-permute-start.2) | collective-permute-done | bytes 262176 | tf_op jit(solution)/shard_map/ppermute | solution.py:412
  21.7 2.8 %collective-permute-done.3.refs_3_ = f32[128,512]{1,0:T(8,128)S(1)} collective-permute-done((f32[128,512]{1,0:T(8,128)S(1)}, f32[128,512]{1,0:T(8,128)S(1)}, u32[]{:S(2)}, u32[]{:S(2)}) %collective-permute-start.3) | collective-permute-done | bytes 262176 | tf_op jit(solution)/shard_map/ppermute | solution.py:412
  24.5 5.0 %first_round.1 = (f32[64,2048]{1,0:T(8,128)S(1)}, f32[64,1024]{1,0:T(8,128)S(1)}, f32[64,1024]{1,0:T(8,128)S(1)}, f32[64,1280]{1,0:T(8,128)S(1)}, f32[64,1536]{1,0:T(8,128)S(1)}, /*index=5*/f32[64,1280]{1,0:T(8,128)S(1)}) custom-call(f32[128,512]{1,0:T(8,128)S(1)} %collective-permute-done.refs_0_, f32[128,512]{1,0:T(8,128)S(1)} %collective-permute-done.1.refs_1_, ...), custom_call_target="tpu_custom_call" | custom-call | tf_op jit(solution)/shard_map/first_round/pallas_call | solution.py:423
  29.5 2.4 %collective-permute-start.7 = (f32[64,1024]{1,0:T(8,128)S(1)}, f32[64,1024]{1,0:T(8,128)S(1)}, u32[]{:S(2)}, u32[]{:S(2)}) collective-permute-start(f32[64,1024]{1,0:T(8,128)S(1)} %get-tuple-element.34.refs_7_), channel_id=1, source_target_pairs={{16,14},{9,15},{18,20},{11,13},{20,18},{13,11},{22,24},{7,1},{24,2... | collective-permute-start | bytes 786440 | tf_op jit(solution)/shard_map/ppermute | solution.py:435
  33.5 7.3 %collective-permute-start.10 = (f32[64,1536]{1,0:T(8,128)S(1)}, f32[64,1536]{1,0:T(8,128)S(1)}, u32[]{:S(2)}, u32[]{:S(2)}) collective-permute-start(f32[64,1536]{1,0:T(8,128)S(1)} %get-tuple-element.37.refs_10_), channel_id=1, source_target_pairs={{10,8},{19,17},{12,14},{21,15},{14,12},{15,21},{16,18},{9,11},{18,... | collective-permute-start | bytes 1179656 | tf_op jit(solution)/shard_map/ppermute | solution.py:435
  40.9 3.9 %collective-permute-start.11 = (f32[64,1280]{1,0:T(8,128)S(1)}, f32[64,1280]{1,0:T(8,128)S(1)}, u32[]{:S(2)}, u32[]{:S(2)}) collective-permute-start(f32[64,1280]{1,0:T(8,128)S(1)} %get-tuple-element.38.refs_11_), channel_id=1, source_target_pairs={{22,20},{7,13},{24,26},{1,3},{26,24},{3,1},{28,30},{5,31},{30,28},... | collective-permute-start | bytes 983048 | tf_op jit(solution)/shard_map/ppermute | solution.py:435
  44.8 2.8 %collective-permute-done.7.refs_1_ = f32[64,1024]{1,0:T(8,128)S(1)} collective-permute-done((f32[64,1024]{1,0:T(8,128)S(1)}, f32[64,1024]{1,0:T(8,128)S(1)}, u32[]{:S(2)}, u32[]{:S(2)}) %collective-permute-start.7) | collective-permute-done | bytes 262176 | tf_op jit(solution)/shard_map/ppermute | solution.py:435
  47.6 1.9 %collective-permute-start.8 = (f32[64,1024]{1,0:T(8,128)S(1)}, f32[64,1024]{1,0:T(8,128)S(1)}, u32[]{:S(2)}, u32[]{:S(2)}) collective-permute-start(f32[64,1024]{1,0:T(8,128)S(1)} %get-tuple-element.35.refs_8_), channel_id=1, source_target_pairs={{24,22},{1,7},{26,28},{3,5},{28,26},{5,3},{30,31},{31,30}} | collective-permute-start | bytes 786440 | tf_op jit(solution)/shard_map/ppermute | solution.py:435
  49.5 6.5 %collective-permute-done.8.refs_2_ = f32[64,1024]{1,0:T(8,128)S(1)} collective-permute-done((f32[64,1024]{1,0:T(8,128)S(1)}, f32[64,1024]{1,0:T(8,128)S(1)}, u32[]{:S(2)}, u32[]{:S(2)}) %collective-permute-start.8) | collective-permute-done | bytes 262176 | tf_op jit(solution)/shard_map/ppermute | solution.py:435
  57.7 6.4 %collective-permute-done.11.refs_5_ = f32[64,1280]{1,0:T(8,128)S(1)} collective-permute-done((f32[64,1280]{1,0:T(8,128)S(1)}, f32[64,1280]{1,0:T(8,128)S(1)}, u32[]{:S(2)}, u32[]{:S(2)}) %collective-permute-start.11) | collective-permute-done | bytes 327712 | tf_op jit(solution)/shard_map/ppermute | solution.py:435
  64.1 12.0 %middle_rounds.1 = (f32[64,2304]{1,0:T(8,128)S(1)}, f32[64,1024]{1,0:T(8,128)S(1)}, f32[64,768]{1,0:T(8,128)S(1)}, f32[64,2304]{1,0:T(8,128)S(1)}, f32[64,1024]{1,0:T(8,128)S(1)}, /*index=5*/f32[64,768]{1,0:T(8,128)S(1)}) custom-call(f32[64,2048]{1,0:T(8,128)S(1)} %collective-permute-done.6.refs_0_, f32[64,1024]{1,0:T(8,128)S(1)} %collective-permute-done.7.refs_1_, ...), custom_call_target="tpu_custom_call" | custom-call | tf_op jit(solution)/shard_map/middle_rounds/pallas_call | solution.py:445
  76.2 1.9 %collective-permute-start.12 = (f32[64,2304]{1,0:T(8,128)S(1)}, f32[64,2304]{1,0:T(8,128)S(1)}, u32[]{:S(2)}, u32[]{:S(2)}) collective-permute-start(f32[64,2304]{1,0:T(8,128)S(1)} %get-tuple-element.39), channel_id=1, source_target_pairs={{0,0},{25,2},{2,1},{27,4},{4,3},{29,6},{6,5},{23,8},{8,7},{17,10},... | collective-permute-start | bytes 1769480 | tf_op jit(solution)/shard_map/ppermute | solution.py:457
  78.2 2.5 %collective-permute-start.14 = (f32[64,768]{1,0:T(8,128)S(1)}, f32[64,768]{1,0:T(8,128)S(1)}, u32[]{:S(2)}, u32[]{:S(2)}) collective-permute-start(f32[64,768]{1,0:T(8,128)S(1)} %get-tuple-element.41), channel_id=1, source_target_pairs={{24,23},{1,26},{26,25},{3,28},{28,27},{5,30},{30,29},{31,31}} | collective-permute-start | bytes 589832 | tf_op jit(solution)/shard_map/ppermute | solution.py:457
  80.7 1.9 %collective-permute-start.13 = (f32[64,1024]{1,0:T(8,128)S(1)}, f32[64,1024]{1,0:T(8,128)S(1)}, u32[]{:S(2)}, u32[]{:S(2)}) collective-permute-start(f32[64,1024]{1,0:T(8,128)S(1)} %get-tuple-element.40), channel_id=1, source_target_pairs={{16,15},{9,18},{18,17},{11,20},{20,19},{13,22},{22,21},{7,24},{24,... | collective-permute-start | bytes 786440 | tf_op jit(solution)/shard_map/ppermute | solution.py:457
  82.6 1.9 %collective-permute-start.16 = (f32[64,1024]{1,0:T(8,128)S(1)}, f32[64,1024]{1,0:T(8,128)S(1)}, u32[]{:S(2)}, u32[]{:S(2)}) collective-permute-start(f32[64,1024]{1,0:T(8,128)S(1)} %get-tuple-element.43), channel_id=1, source_target_pairs={{16,17},{9,16},{18,19},{11,18},{20,21},{13,20},{22,23},{7,22},{24,... | collective-permute-start | bytes 786440 | tf_op jit(solution)/shard_map/ppermute | solution.py:458
  84.6 6.8 %collective-permute-done.14.refs_2_ = f32[64,768]{1,0:T(8,128)S(1)} collective-permute-done((f32[64,768]{1,0:T(8,128)S(1)}, f32[64,768]{1,0:T(8,128)S(1)}, u32[]{:S(2)}, u32[]{:S(2)}) %collective-permute-start.14) | collective-permute-done | bytes 196640 | tf_op jit(solution)/shard_map/ppermute | solution.py:457
  91.4 1.9 %collective-permute-start.17 = (f32[64,768]{1,0:T(8,128)S(1)}, f32[64,768]{1,0:T(8,128)S(1)}, u32[]{:S(2)}, u32[]{:S(2)}) collective-permute-start(f32[64,768]{1,0:T(8,128)S(1)} %get-tuple-element.44), channel_id=1, source_target_pairs={{24,25},{1,24},{26,27},{3,26},{28,29},{5,28},{30,31},{31,30}} | collective-permute-start | bytes 589832 | tf_op jit(solution)/shard_map/ppermute | solution.py:458
  93.3 11.2 %collective-permute-done.17.refs_5_ = f32[64,768]{1,0:T(8,128)S(1)} collective-permute-done((f32[64,768]{1,0:T(8,128)S(1)}, f32[64,768]{1,0:T(8,128)S(1)}, u32[]{:S(2)}, u32[]{:S(2)}) %collective-permute-start.17) | collective-permute-done | bytes 196640 | tf_op jit(solution)/shard_map/ppermute | solution.py:458
  104.5 5.3 %last_round.1 = f32[4096,128]{1,0:T(8,128)} custom-call(f32[64,2304]{1,0:T(8,128)S(1)} %collective-permute-done.12.refs_0_, f32[64,1024]{1,0:T(8,128)S(1)} %collective-permute-done.13.refs_1_, f32[64,768]{1,0:T(8,128)S(1)} %collective-permute-done.14.refs_2_, f32[64,2304]{1,0:T(8,128)S(1)} %collective-permute-done.15.refs_3_, ...), custom_call_target="tpu_custom_call" | custom-call | tf_op jit(solution)/shard_map/last_round/pallas_call | solution.py:459
  (16 shorter events, 7.7 us)
Async XLA Ops:
  2.1 11.4 %collective-permute-start = (f32[128,512]{1,0:T(8,128)S(1)}, f32[128,512]{1,0:T(8,128)S(1)}, u32[]{:S(2)}, u32[]{:S(2)}) collective-permute-start(f32[128,512]{1,0:T(8,128)S(1)} %get-tuple-element.25), channel_id=1, source_target_pairs={{0,24},{2,26},{4,28},{6,30},{7,31},{8,16},{10,18},{12,20},{14,22},... | collective-permute-start | bytes 786440 | tf_op jit(solution)/shard_map/ppermute | solution.py:412
  3.4 14.5 %collective-permute-start.1 = (f32[128,512]{1,0:T(8,128)S(1)}, f32[128,512]{1,0:T(8,128)S(1)}, u32[]{:S(2)}, u32[]{:S(2)}) collective-permute-start(f32[128,512]{1,0:T(8,128)S(1)} %get-tuple-element.26), channel_id=1, source_target_pairs={{0,24},{1,25},{2,26},{3,27},{4,28},{5,29},{6,30},{7,31},{8,16},{9,... | collective-permute-start | bytes 786440 | tf_op jit(solution)/shard_map/ppermute | solution.py:412
  7.0 14.6 %collective-permute-start.2 = (f32[128,512]{1,0:T(8,128)S(1)}, f32[128,512]{1,0:T(8,128)S(1)}, u32[]{:S(2)}, u32[]{:S(2)}) collective-permute-start(f32[128,512]{1,0:T(8,128)S(1)} %get-tuple-element.27), channel_id=1, source_target_pairs={{0,16},{2,18},{4,20},{6,22},{8,24},{10,26},{12,28},{14,30},{15,31}... | collective-permute-start | bytes 786440 | tf_op jit(solution)/shard_map/ppermute | solution.py:412
  8.3 16.2 %collective-permute-start.3 = (f32[128,512]{1,0:T(8,128)S(1)}, f32[128,512]{1,0:T(8,128)S(1)}, u32[]{:S(2)}, u32[]{:S(2)}) collective-permute-start(f32[128,512]{1,0:T(8,128)S(1)} %get-tuple-element.28), channel_id=1, source_target_pairs={{0,16},{1,17},{2,18},{3,19},{4,20},{5,21},{6,22},{7,23},{8,24},{9,... | collective-permute-start | bytes 786440 | tf_op jit(solution)/shard_map/ppermute | solution.py:412
  11.0 13.4 %collective-permute-start.4 = (f32[128,512]{1,0:T(8,128)S(1)}, f32[128,512]{1,0:T(8,128)S(1)}, u32[]{:S(2)}, u32[]{:S(2)}) collective-permute-start(f32[128,512]{1,0:T(8,128)S(1)} %get-tuple-element.29), channel_id=1, source_target_pairs={{1,9},{3,11},{5,13},{9,1},{11,3},{13,5},{15,7},{16,24},{18,26},{20... | collective-permute-start | bytes 786440 | tf_op jit(solution)/shard_map/ppermute | solution.py:412
  13.5 11.0 %collective-permute-start.5 = (f32[128,512]{1,0:T(8,128)S(1)}, f32[128,512]{1,0:T(8,128)S(1)}, u32[]{:S(2)}, u32[]{:S(2)}) collective-permute-start(f32[128,512]{1,0:T(8,128)S(1)} %get-tuple-element.30), channel_id=1, source_target_pairs={{0,8},{1,9},{2,10},{3,11},{4,12},{5,13},{6,14},{7,15},{8,0},{9,1},... | collective-permute-start | bytes 786440 | tf_op jit(solution)/shard_map/ppermute | solution.py:412
  29.5 18.0 %collective-permute-start.7 = (f32[64,1024]{1,0:T(8,128)S(1)}, f32[64,1024]{1,0:T(8,128)S(1)}, u32[]{:S(2)}, u32[]{:S(2)}) collective-permute-start(f32[64,1024]{1,0:T(8,128)S(1)} %get-tuple-element.34.refs_7_), channel_id=1, source_target_pairs={{16,14},{9,15},{18,20},{11,13},{20,18},{13,11},{22,24},{7,1},{24,2... | collective-permute-start | bytes 786440 | tf_op jit(solution)/shard_map/ppermute | solution.py:435
  31.9 32.3 %collective-permute-start.6 = (f32[64,2048]{1,0:T(8,128)S(1)}, f32[64,2048]{1,0:T(8,128)S(1)}, u32[]{:S(2)}, u32[]{:S(2)}) collective-permute-start(f32[64,2048]{1,0:T(8,128)S(1)} %get-tuple-element.33.refs_6_), channel_id=1, source_target_pairs={{0,25},{25,0},{2,4},{27,29},{4,2},{29,27},{6,8},{23,17},{8,6},{17,... | collective-permute-start | bytes 1572872 | tf_op jit(solution)/shard_map/ppermute | solution.py:435
  33.5 30.6 %collective-permute-start.10 = (f32[64,1536]{1,0:T(8,128)S(1)}, f32[64,1536]{1,0:T(8,128)S(1)}, u32[]{:S(2)}, u32[]{:S(2)}) collective-permute-start(f32[64,1536]{1,0:T(8,128)S(1)} %get-tuple-element.37.refs_10_), channel_id=1, source_target_pairs={{10,8},{19,17},{12,14},{21,15},{14,12},{15,21},{16,18},{9,11},{18,... | collective-permute-start | bytes 1179656 | tf_op jit(solution)/shard_map/ppermute | solution.py:435
  40.8 16.9 %collective-permute-start.9 = (f32[64,1280]{1,0:T(8,128)S(1)}, f32[64,1280]{1,0:T(8,128)S(1)}, u32[]{:S(2)}, u32[]{:S(2)}) collective-permute-start(f32[64,1280]{1,0:T(8,128)S(1)} %get-tuple-element.36.refs_9_), channel_id=1, source_target_pairs={{0,2},{25,27},{2,0},{27,25},{4,6},{29,23},{6,4},{23,29},{8,10},{17... | collective-permute-start | bytes 983048 | tf_op jit(solution)/shard_map/ppermute | solution.py:435
  40.9 23.3 %collective-permute-start.11 = (f32[64,1280]{1,0:T(8,128)S(1)}, f32[64,1280]{1,0:T(8,128)S(1)}, u32[]{:S(2)}, u32[]{:S(2)}) collective-permute-start(f32[64,1280]{1,0:T(8,128)S(1)} %get-tuple-element.38.refs_11_), channel_id=1, source_target_pairs={{22,20},{7,13},{24,26},{1,3},{26,24},{3,1},{28,30},{5,31},{30,28},... | collective-permute-start | bytes 983048 | tf_op jit(solution)/shard_map/ppermute | solution.py:435
  47.6 8.4 %collective-permute-start.8 = (f32[64,1024]{1,0:T(8,128)S(1)}, f32[64,1024]{1,0:T(8,128)S(1)}, u32[]{:S(2)}, u32[]{:S(2)}) collective-permute-start(f32[64,1024]{1,0:T(8,128)S(1)} %get-tuple-element.35.refs_8_), channel_id=1, source_target_pairs={{24,22},{1,7},{26,28},{3,5},{28,26},{5,3},{30,31},{31,30}} | collective-permute-start | bytes 786440 | tf_op jit(solution)/shard_map/ppermute | solution.py:435
  76.2 28.3 %collective-permute-start.12 = (f32[64,2304]{1,0:T(8,128)S(1)}, f32[64,2304]{1,0:T(8,128)S(1)}, u32[]{:S(2)}, u32[]{:S(2)}) collective-permute-start(f32[64,2304]{1,0:T(8,128)S(1)} %get-tuple-element.39), channel_id=1, source_target_pairs={{0,0},{25,2},{2,1},{27,4},{4,3},{29,6},{6,5},{23,8},{8,7},{17,10},... | collective-permute-start | bytes 1769480 | tf_op jit(solution)/shard_map/ppermute | solution.py:457
  78.1 26.4 %collective-permute-start.15 = (f32[64,2304]{1,0:T(8,128)S(1)}, f32[64,2304]{1,0:T(8,128)S(1)}, u32[]{:S(2)}, u32[]{:S(2)}) collective-permute-start(f32[64,2304]{1,0:T(8,128)S(1)} %get-tuple-element.42), channel_id=1, source_target_pairs={{0,1},{25,0},{2,3},{27,2},{4,5},{29,4},{6,7},{23,6},{8,9},{17,8},{... | collective-permute-start | bytes 1769480 | tf_op jit(solution)/shard_map/ppermute | solution.py:458
  78.2 13.2 %collective-permute-start.14 = (f32[64,768]{1,0:T(8,128)S(1)}, f32[64,768]{1,0:T(8,128)S(1)}, u32[]{:S(2)}, u32[]{:S(2)}) collective-permute-start(f32[64,768]{1,0:T(8,128)S(1)} %get-tuple-element.41), channel_id=1, source_target_pairs={{24,23},{1,26},{26,25},{3,28},{28,27},{5,30},{30,29},{31,31}} | collective-permute-start | bytes 589832 | tf_op jit(solution)/shard_map/ppermute | solution.py:457
  80.7 23.8 %collective-permute-start.13 = (f32[64,1024]{1,0:T(8,128)S(1)}, f32[64,1024]{1,0:T(8,128)S(1)}, u32[]{:S(2)}, u32[]{:S(2)}) collective-permute-start(f32[64,1024]{1,0:T(8,128)S(1)} %get-tuple-element.40), channel_id=1, source_target_pairs={{16,15},{9,18},{18,17},{11,20},{20,19},{13,22},{22,21},{7,24},{24,... | collective-permute-start | bytes 786440 | tf_op jit(solution)/shard_map/ppermute | solution.py:457
  82.6 21.9 %collective-permute-start.16 = (f32[64,1024]{1,0:T(8,128)S(1)}, f32[64,1024]{1,0:T(8,128)S(1)}, u32[]{:S(2)}, u32[]{:S(2)}) collective-permute-start(f32[64,1024]{1,0:T(8,128)S(1)} %get-tuple-element.43), channel_id=1, source_target_pairs={{16,17},{9,16},{18,19},{11,18},{20,21},{13,20},{22,23},{7,22},{24,... | collective-permute-start | bytes 786440 | tf_op jit(solution)/shard_map/ppermute | solution.py:458
  91.4 13.1 %collective-permute-start.17 = (f32[64,768]{1,0:T(8,128)S(1)}, f32[64,768]{1,0:T(8,128)S(1)}, u32[]{:S(2)}, u32[]{:S(2)}) collective-permute-start(f32[64,768]{1,0:T(8,128)S(1)} %get-tuple-element.44), channel_id=1, source_target_pairs={{24,25},{1,24},{26,27},{3,26},{28,29},{5,28},{30,31},{31,30}} | collective-permute-start | bytes 589832 | tf_op jit(solution)/shard_map/ppermute | solution.py:458

commit v4 on v1

--- a/solution.py
+++ b/solution.py
@@ -19,6 +19,7 @@
 NEAR_CUTS = (10, 22)
 FAR_CUTS = (16, 24)
 LAST_CUTS = (18, 26)
+ON_CUTS = (18,)
 PIECES = 2
 
 damping_ratio = 0.01
@@ -267,10 +268,10 @@
 
 
 def middle_kernel(near_count, *refs):
-    sizes = len(LAST_CUTS) + 1
+    off_count, on_count = len(LAST_CUTS) + 1, len(ON_CUTS) + 1
     near_ref, far_ref = refs[-2:]
-    off_outs, on_outs = refs[-2 - 2 * sizes : -2 - sizes], refs[-2 - sizes : -2]
-    halves = refs[: -2 - 2 * sizes]
+    off_outs, on_outs = refs[-2 - on_count - off_count : -2 - on_count], refs[-2 - on_count : -2]
+    halves = refs[: -2 - on_count - off_count]
     in_refs, own_refs = halves[: len(halves) // 2], halves[len(halves) // 2 :]
     far_in, near_in = in_refs[:-near_count], in_refs[-near_count:]
     second, first = own_refs[:-near_count], own_refs[-near_count:]
@@ -306,8 +307,8 @@
 
 def last_kernel(*refs):
     out_ref, split_ref, buffer, done = refs[-4:]
-    sizes = (len(refs) - 4) // 2
-    off_in, on_in = refs[:sizes], refs[sizes:-4]
+    off_count = len(LAST_CUTS) + 1
+    off_in, on_in = refs[:off_count], refs[off_count:-4]
     half = off_in[0].shape[0]
     odd = jnp.bitwise_and(lax.axis_index("col"), 1)
     load_rows(split_ref, off_in, pl.multiple_of(odd * half, half))
@@ -436,29 +437,31 @@
 
     far = [swapped(value, start, 1) for value, start in zip(far, far_starts)]
     near = [swapped(value, start, 0) for value, start in zip(near, near_starts)]
-    last_starts = [0] + [cut * unit for cut in LAST_CUTS]
-    sizes = len(last_starts)
+    off_starts = [0] + [cut * unit for cut in LAST_CUTS]
+    on_starts = [0] + [cut * unit for cut in ON_CUTS]
+    off_count = len(off_starts)
     last_halves = [
         jax.ShapeDtypeStruct((half, end - start), jnp.float32)
-        for start, end in zip(last_starts, last_starts[1:] + [length])
+        for starts in (off_starts, on_starts)
+        for start, end in zip(starts, starts[1:] + [length])
     ]
     last = pl.pallas_call(
         functools.partial(middle_kernel, near_count),
         in_specs=in_vmem(2 * len(halves)),
-        out_specs=in_vmem(2 * sizes),
-        out_shape=last_halves * 2,
+        out_specs=in_vmem(len(last_halves)),
+        out_shape=last_halves,
         scratch_shapes=[split] * 2,
         compiler_params=more_params,
         name="middle_rounds",
     )(*far, *near, *moved)
-    off, on = list(last[:sizes]), list(last[sizes:])
-    for place, start in enumerate(last_starts):
-        off_pairs, on_pairs = last_pairs(start, width, count, columns)
-        off[place] = lax.ppermute(off[place], axes, off_pairs)
-        on[place] = lax.ppermute(on[place], axes, on_pairs)
+    off, on = list(last[:off_count]), list(last[off_count:])
+    for values, starts, side in ((off, off_starts, 0), (on, on_starts, 1)):
+        for place, start in enumerate(starts):
+            pairs = last_pairs(start, width, count, columns)[side]
+            values[place] = lax.ppermute(values[place], axes, pairs)
     return pl.pallas_call(
         last_kernel,
-        in_specs=in_vmem(2 * sizes),
+        in_specs=in_vmem(len(last_halves)),
         out_specs=pl.BlockSpec(memory_space=pltpu.HBM),
         out_shape=jax.ShapeDtypeStruct((length, width), jnp.float32),
         scratch_shapes=[

time: 108 us -> 108 us (level)
    ppermute x6 -> x5, waiting for transfers between devices: 17.8 us -> 18.8 us  [per_device(): values[place] = lax.ppermute(values[place], axes, pairs)]
    ppermute x6 -> x5, starting transfers between devices: 10.5 us -> 9.53 us  [per_device(): values[place] = lax.ppermute(values[place], axes, pairs)]
  transfers between devices with their start and end apart: 18 -> 17, of which waited for: 9 -> 9; matrix products, arithmetic and copies ran while one was open for 0% -> 0% of each run, Pallas kernels for 0% -> 0%
where the time goes in v4:
time: 108 us
  waiting for transfers between devices  45.6 us (42%)
  starting transfers between devices  39.6 us (37%)
  Pallas kernels  22.2 us (21%)
    ppermute x5, waiting for transfers between devices, per_device(): values[place] = lax.ppermute(values[place], axes, pairs)  18.8 us
    ppermute x6, waiting for transfers between devices, swapped(): lax.ppermute(value, axes, swap_pairs(first_row, width, count, columns)[si...  17.4 us
    ppermute x6, starting transfers between devices, swapped(): lax.ppermute(value, axes, swap_pairs(first_row, width, count, columns)[si...  17.2 us
    ppermute x6, starting transfers between devices, per_device(): received[place] = lax.ppermute(chunks[place], axes, pairs)  12.9 us
    pallas_call x1, Pallas kernels, per_device(): pl.pallas_call(functools.partial(middle_kernel, near_count), in_specs=in_...  10.7 us
    ppermute x5, starting transfers between devices, per_device(): values[place] = lax.ppermute(values[place], axes, pairs)  9.53 us
    ppermute x6, waiting for transfers between devices, per_device(): received[place] = lax.ppermute(chunks[place], axes, pairs)  9.45 us
    pallas_call x1, Pallas kernels, per_device(): pl.pallas_call(last_kernel, in_specs=in_vmem(len(last_halves)), out_specs...  4.86 us
  transfers between devices with their start and end apart: 17, of which 9 were waited for; matrix products, arithmetic and copies ran while one was open for 0% of the time, Pallas kernels for 0%

profile of v4, /device:TPU:22, one launch (start us, length us, event | category | flops | bytes accessed | tf_op | source)
XLA Modules:
  0.0 107.8 jit_solution(2841469917923558696)
XLA Ops:
  0.0 2.1 %prepare.1 = (f32[128,512]{1,0:T(8,128)S(1)}, f32[128,512]{1,0:T(8,128)S(1)}, f32[128,512]{1,0:T(8,128)S(1)}, f32[128,512]{1,0:T(8,128)S(1)}, f32[128,512]{1,0:T...) custom-call(f32[8,512,128]{2,1,0:T(8,128)} %bitcast.1), custom_call_target="tpu_custom_call" | custom-call | tf_op jit(solution)/shard_map/prepare/pallas_call | solution.py:397
  3.4 3.6 %collective-permute-start.1 = (f32[128,512]{1,0:T(8,128)S(1)}, f32[128,512]{1,0:T(8,128)S(1)}, u32[]{:S(2)}, u32[]{:S(2)}) collective-permute-start(f32[128,512]{1,0:T(8,128)S(1)} %get-tuple-element.25), channel_id=1, source_target_pairs={{0,24},{1,25},{2,26},{3,27},{4,28},{5,29},{6,30},{7,31},{8,16},{9,... | collective-permute-start | bytes 786440 | tf_op jit(solution)/shard_map/ppermute | solution.py:413
  8.3 2.7 %collective-permute-start.3 = (f32[128,512]{1,0:T(8,128)S(1)}, f32[128,512]{1,0:T(8,128)S(1)}, u32[]{:S(2)}, u32[]{:S(2)}) collective-permute-start(f32[128,512]{1,0:T(8,128)S(1)} %get-tuple-element.27), channel_id=1, source_target_pairs={{0,16},{1,17},{2,18},{3,19},{4,20},{5,21},{6,22},{7,23},{8,24},{9,... | collective-permute-start | bytes 786440 | tf_op jit(solution)/shard_map/ppermute | solution.py:413
  11.0 2.4 %collective-permute-start.4 = (f32[128,512]{1,0:T(8,128)S(1)}, f32[128,512]{1,0:T(8,128)S(1)}, u32[]{:S(2)}, u32[]{:S(2)}) collective-permute-start(f32[128,512]{1,0:T(8,128)S(1)} %get-tuple-element.28), channel_id=1, source_target_pairs={{1,9},{3,11},{5,13},{9,1},{11,3},{13,5},{15,7},{16,24},{18,26},{20... | collective-permute-start | bytes 786440 | tf_op jit(solution)/shard_map/ppermute | solution.py:413
  15.0 2.9 %collective-permute-done.1.refs_1_ = f32[128,512]{1,0:T(8,128)S(1)} collective-permute-done((f32[128,512]{1,0:T(8,128)S(1)}, f32[128,512]{1,0:T(8,128)S(1)}, u32[]{:S(2)}, u32[]{:S(2)}) %collective-permute-start.1) | collective-permute-done | bytes 262176 | tf_op jit(solution)/shard_map/ppermute | solution.py:413
  18.0 3.7 %collective-permute-done.2.refs_2_ = f32[128,512]{1,0:T(8,128)S(1)} collective-permute-done((f32[128,512]{1,0:T(8,128)S(1)}, f32[128,512]{1,0:T(8,128)S(1)}, u32[]{:S(2)}, u32[]{:S(2)}) %collective-permute-start.2) | collective-permute-done | bytes 262176 | tf_op jit(solution)/shard_map/ppermute | solution.py:413
  21.7 2.8 %collective-permute-done.3.refs_3_ = f32[128,512]{1,0:T(8,128)S(1)} collective-permute-done((f32[128,512]{1,0:T(8,128)S(1)}, f32[128,512]{1,0:T(8,128)S(1)}, u32[]{:S(2)}, u32[]{:S(2)}) %collective-permute-start.3) | collective-permute-done | bytes 262176 | tf_op jit(solution)/shard_map/ppermute | solution.py:413
  24.5 4.6 %first_round.1 = (f32[64,2048]{1,0:T(8,128)S(1)}, f32[64,1024]{1,0:T(8,128)S(1)}, f32[64,1024]{1,0:T(8,128)S(1)}, f32[64,1280]{1,0:T(8,128)S(1)}, f32[64,1536]{1,0:T(8,128)S(1)}, /*index=5*/f32[64,1280]{1,0:T(8,128)S(1)}) custom-call(f32[128,512]{1,0:T(8,128)S(1)} %collective-permute-done.refs_0_, f32[128,512]{1,0:T(8,128)S(1)} %collective-permute-done.1.refs_1_, ...), custom_call_target="tpu_custom_call" | custom-call | tf_op jit(solution)/shard_map/first_round/pallas_call | solution.py:424
  29.1 2.4 %collective-permute-start.7 = (f32[64,1024]{1,0:T(8,128)S(1)}, f32[64,1024]{1,0:T(8,128)S(1)}, u32[]{:S(2)}, u32[]{:S(2)}) collective-permute-start(f32[64,1024]{1,0:T(8,128)S(1)} %get-tuple-element.33.refs_7_), channel_id=1, source_target_pairs={{16,14},{9,15},{18,20},{11,13},{20,18},{13,11},{22,24},{7,1},{24,2... | collective-permute-start | bytes 786440 | tf_op jit(solution)/shard_map/ppermute | solution.py:436
  33.1 7.3 %collective-permute-start.10 = (f32[64,1536]{1,0:T(8,128)S(1)}, f32[64,1536]{1,0:T(8,128)S(1)}, u32[]{:S(2)}, u32[]{:S(2)}) collective-permute-start(f32[64,1536]{1,0:T(8,128)S(1)} %get-tuple-element.36.refs_10_), channel_id=1, source_target_pairs={{10,8},{19,17},{12,14},{21,15},{14,12},{15,21},{16,18},{9,11},{18,... | collective-permute-start | bytes 1179656 | tf_op jit(solution)/shard_map/ppermute | solution.py:436
  40.5 3.9 %collective-permute-start.11 = (f32[64,1280]{1,0:T(8,128)S(1)}, f32[64,1280]{1,0:T(8,128)S(1)}, u32[]{:S(2)}, u32[]{:S(2)}) collective-permute-start(f32[64,1280]{1,0:T(8,128)S(1)} %get-tuple-element.37.refs_11_), channel_id=1, source_target_pairs={{22,20},{7,13},{24,26},{1,3},{26,24},{3,1},{28,30},{5,31},{30,28},... | collective-permute-start | bytes 983048 | tf_op jit(solution)/shard_map/ppermute | solution.py:436
  44.4 2.8 %collective-permute-done.7.refs_1_ = f32[64,1024]{1,0:T(8,128)S(1)} collective-permute-done((f32[64,1024]{1,0:T(8,128)S(1)}, f32[64,1024]{1,0:T(8,128)S(1)}, u32[]{:S(2)}, u32[]{:S(2)}) %collective-permute-start.7) | collective-permute-done | bytes 262176 | tf_op jit(solution)/shard_map/ppermute | solution.py:436
  47.1 1.9 %collective-permute-start.8 = (f32[64,1024]{1,0:T(8,128)S(1)}, f32[64,1024]{1,0:T(8,128)S(1)}, u32[]{:S(2)}, u32[]{:S(2)}) collective-permute-start(f32[64,1024]{1,0:T(8,128)S(1)} %get-tuple-element.34.refs_8_), channel_id=1, source_target_pairs={{24,22},{1,7},{26,28},{3,5},{28,26},{5,3},{30,31},{31,30}} | collective-permute-start | bytes 786440 | tf_op jit(solution)/shard_map/ppermute | solution.py:436
  49.0 6.5 %collective-permute-done.8.refs_2_ = f32[64,1024]{1,0:T(8,128)S(1)} collective-permute-done((f32[64,1024]{1,0:T(8,128)S(1)}, f32[64,1024]{1,0:T(8,128)S(1)}, u32[]{:S(2)}, u32[]{:S(2)}) %collective-permute-start.8) | collective-permute-done | bytes 262176 | tf_op jit(solution)/shard_map/ppermute | solution.py:436
  55.6 1.7 %collective-permute-done.9.refs_3_ = f32[64,1280]{1,0:T(8,128)S(1)} collective-permute-done((f32[64,1280]{1,0:T(8,128)S(1)}, f32[64,1280]{1,0:T(8,128)S(1)}, u32[]{:S(2)}, u32[]{:S(2)}) %collective-permute-start.9) | collective-permute-done | bytes 327712 | tf_op jit(solution)/shard_map/ppermute | solution.py:436
  57.3 6.4 %collective-permute-done.11.refs_5_ = f32[64,1280]{1,0:T(8,128)S(1)} collective-permute-done((f32[64,1280]{1,0:T(8,128)S(1)}, f32[64,1280]{1,0:T(8,128)S(1)}, u32[]{:S(2)}, u32[]{:S(2)}) %collective-permute-start.11) | collective-permute-done | bytes 327712 | tf_op jit(solution)/shard_map/ppermute | solution.py:436
  63.7 10.7 %middle_rounds.1 = (f32[64,2304]{1,0:T(8,128)S(1)}, f32[64,1024]{1,0:T(8,128)S(1)}, f32[64,768]{1,0:T(8,128)S(1)}, f32[64,2304]{1,0:T(8,128)S(1)}, f32[64,1792]{1,0:T(8,128)S(1)}) custom-call(f32[64,2048]{1,0:T(8,128)S(1)} %collective-permute-done.6.refs_0_, f32[64,1024]{1,0:T(8,128)S(1)} %collective-permute-done.7.refs_1_, ...), custom_call_target="tpu_custom_call" | custom-call | tf_op jit(solution)/shard_map/middle_rounds/pallas_call | solution.py:448
  74.4 1.9 %collective-permute-start.12 = (f32[64,2304]{1,0:T(8,128)S(1)}, f32[64,2304]{1,0:T(8,128)S(1)}, u32[]{:S(2)}, u32[]{:S(2)}) collective-permute-start(f32[64,2304]{1,0:T(8,128)S(1)} %get-tuple-element.38), channel_id=1, source_target_pairs={{0,0},{25,2},{2,1},{27,4},{4,3},{29,6},{6,5},{23,8},{8,7},{17,10},... | collective-permute-start | bytes 1769480 | tf_op jit(solution)/shard_map/ppermute | solution.py:461
  76.4 3.5 %collective-permute-start.16 = (f32[64,1792]{1,0:T(8,128)S(1)}, f32[64,1792]{1,0:T(8,128)S(1)}, u32[]{:S(2)}, u32[]{:S(2)}) collective-permute-start(f32[64,1792]{1,0:T(8,128)S(1)} %get-tuple-element.42), channel_id=1, source_target_pairs={{16,17},{9,16},{18,19},{11,18},{20,21},{13,20},{22,23},{7,22},{24,... | collective-permute-start | bytes 1376264 | tf_op jit(solution)/shard_map/ppermute | solution.py:461
  79.9 1.9 %collective-permute-start.13 = (f32[64,1024]{1,0:T(8,128)S(1)}, f32[64,1024]{1,0:T(8,128)S(1)}, u32[]{:S(2)}, u32[]{:S(2)}) collective-permute-start(f32[64,1024]{1,0:T(8,128)S(1)} %get-tuple-element.39), channel_id=1, source_target_pairs={{16,15},{9,18},{18,17},{11,20},{20,19},{13,22},{22,21},{7,24},{24,... | collective-permute-start | bytes 786440 | tf_op jit(solution)/shard_map/ppermute | solution.py:461
  81.9 2.1 %collective-permute-start.14 = (f32[64,768]{1,0:T(8,128)S(1)}, f32[64,768]{1,0:T(8,128)S(1)}, u32[]{:S(2)}, u32[]{:S(2)}) collective-permute-start(f32[64,768]{1,0:T(8,128)S(1)} %get-tuple-element.40), channel_id=1, source_target_pairs={{24,23},{1,26},{26,25},{3,28},{28,27},{5,30},{30,29},{31,31}} | collective-permute-start | bytes 589832 | tf_op jit(solution)/shard_map/ppermute | solution.py:461
  84.0 8.5 %collective-permute-done.14.refs_2_ = f32[64,768]{1,0:T(8,128)S(1)} collective-permute-done((f32[64,768]{1,0:T(8,128)S(1)}, f32[64,768]{1,0:T(8,128)S(1)}, u32[]{:S(2)}, u32[]{:S(2)}) %collective-permute-start.14) | collective-permute-done | bytes 196640 | tf_op jit(solution)/shard_map/ppermute | solution.py:461
  92.4 10.3 %collective-permute-done.16.refs_4_ = f32[64,1792]{1,0:T(8,128)S(1)} collective-permute-done((f32[64,1792]{1,0:T(8,128)S(1)}, f32[64,1792]{1,0:T(8,128)S(1)}, u32[]{:S(2)}, u32[]{:S(2)}) %collective-permute-start.16) | collective-permute-done | bytes 458784 | tf_op jit(solution)/shard_map/ppermute | solution.py:461
  102.7 4.9 %last_round.1 = f32[4096,128]{1,0:T(8,128)} custom-call(f32[64,2304]{1,0:T(8,128)S(1)} %collective-permute-done.12.refs_0_, f32[64,1024]{1,0:T(8,128)S(1)} %collective-permute-done.13.refs_1_, f32[64,768]{1,0:T(8,128)S(1)} %collective-permute-done.14.refs_2_, f32[64,2304]{1,0:T(8,128)S(1)} %collective-permute-done.15.refs_3_, ...), custom_call_target="tpu_custom_call" | custom-call | tf_op jit(solution)/shard_map/last_round/pallas_call | solution.py:462
  (14 shorter events, 5.9 us)
Async XLA Ops:
  2.1 11.4 %collective-permute-start = (f32[128,512]{1,0:T(8,128)S(1)}, f32[128,512]{1,0:T(8,128)S(1)}, u32[]{:S(2)}, u32[]{:S(2)}) collective-permute-start(f32[128,512]{1,0:T(8,128)S(1)} %get-tuple-element.24), channel_id=1, source_target_pairs={{0,24},{2,26},{4,28},{6,30},{7,31},{8,16},{10,18},{12,20},{14,22},... | collective-permute-start | bytes 786440 | tf_op jit(solution)/shard_map/ppermute | solution.py:413
  3.4 14.5 %collective-permute-start.1 = (f32[128,512]{1,0:T(8,128)S(1)}, f32[128,512]{1,0:T(8,128)S(1)}, u32[]{:S(2)}, u32[]{:S(2)}) collective-permute-start(f32[128,512]{1,0:T(8,128)S(1)} %get-tuple-element.25), channel_id=1, source_target_pairs={{0,24},{1,25},{2,26},{3,27},{4,28},{5,29},{6,30},{7,31},{8,16},{9,... | collective-permute-start | bytes 786440 | tf_op jit(solution)/shard_map/ppermute | solution.py:413
  7.0 14.6 %collective-permute-start.2 = (f32[128,512]{1,0:T(8,128)S(1)}, f32[128,512]{1,0:T(8,128)S(1)}, u32[]{:S(2)}, u32[]{:S(2)}) collective-permute-start(f32[128,512]{1,0:T(8,128)S(1)} %get-tuple-element.26), channel_id=1, source_target_pairs={{0,16},{2,18},{4,20},{6,22},{8,24},{10,26},{12,28},{14,30},{15,31}... | collective-permute-start | bytes 786440 | tf_op jit(solution)/shard_map/ppermute | solution.py:413
  8.3 16.2 %collective-permute-start.3 = (f32[128,512]{1,0:T(8,128)S(1)}, f32[128,512]{1,0:T(8,128)S(1)}, u32[]{:S(2)}, u32[]{:S(2)}) collective-permute-start(f32[128,512]{1,0:T(8,128)S(1)} %get-tuple-element.27), channel_id=1, source_target_pairs={{0,16},{1,17},{2,18},{3,19},{4,20},{5,21},{6,22},{7,23},{8,24},{9,... | collective-permute-start | bytes 786440 | tf_op jit(solution)/shard_map/ppermute | solution.py:413
  11.0 13.4 %collective-permute-start.4 = (f32[128,512]{1,0:T(8,128)S(1)}, f32[128,512]{1,0:T(8,128)S(1)}, u32[]{:S(2)}, u32[]{:S(2)}) collective-permute-start(f32[128,512]{1,0:T(8,128)S(1)} %get-tuple-element.28), channel_id=1, source_target_pairs={{1,9},{3,11},{5,13},{9,1},{11,3},{13,5},{15,7},{16,24},{18,26},{20... | collective-permute-start | bytes 786440 | tf_op jit(solution)/shard_map/ppermute | solution.py:413
  13.5 11.0 %collective-permute-start.5 = (f32[128,512]{1,0:T(8,128)S(1)}, f32[128,512]{1,0:T(8,128)S(1)}, u32[]{:S(2)}, u32[]{:S(2)}) collective-permute-start(f32[128,512]{1,0:T(8,128)S(1)} %get-tuple-element.29), channel_id=1, source_target_pairs={{0,8},{1,9},{2,10},{3,11},{4,12},{5,13},{6,14},{7,15},{8,0},{9,1},... | collective-permute-start | bytes 786440 | tf_op jit(solution)/shard_map/ppermute | solution.py:413
  29.1 18.0 %collective-permute-start.7 = (f32[64,1024]{1,0:T(8,128)S(1)}, f32[64,1024]{1,0:T(8,128)S(1)}, u32[]{:S(2)}, u32[]{:S(2)}) collective-permute-start(f32[64,1024]{1,0:T(8,128)S(1)} %get-tuple-element.33.refs_7_), channel_id=1, source_target_pairs={{16,14},{9,15},{18,20},{11,13},{20,18},{13,11},{22,24},{7,1},{24,2... | collective-permute-start | bytes 786440 | tf_op jit(solution)/shard_map/ppermute | solution.py:436
  31.4 32.3 %collective-permute-start.6 = (f32[64,2048]{1,0:T(8,128)S(1)}, f32[64,2048]{1,0:T(8,128)S(1)}, u32[]{:S(2)}, u32[]{:S(2)}) collective-permute-start(f32[64,2048]{1,0:T(8,128)S(1)} %get-tuple-element.32.refs_6_), channel_id=1, source_target_pairs={{0,25},{25,0},{2,4},{27,29},{4,2},{29,27},{6,8},{23,17},{8,6},{17,... | collective-permute-start | bytes 1572872 | tf_op jit(solution)/shard_map/ppermute | solution.py:436
  33.1 30.6 %collective-permute-start.10 = (f32[64,1536]{1,0:T(8,128)S(1)}, f32[64,1536]{1,0:T(8,128)S(1)}, u32[]{:S(2)}, u32[]{:S(2)}) collective-permute-start(f32[64,1536]{1,0:T(8,128)S(1)} %get-tuple-element.36.refs_10_), channel_id=1, source_target_pairs={{10,8},{19,17},{12,14},{21,15},{14,12},{15,21},{16,18},{9,11},{18,... | collective-permute-start | bytes 1179656 | tf_op jit(solution)/shard_map/ppermute | solution.py:436
  40.4 16.9 %collective-permute-start.9 = (f32[64,1280]{1,0:T(8,128)S(1)}, f32[64,1280]{1,0:T(8,128)S(1)}, u32[]{:S(2)}, u32[]{:S(2)}) collective-permute-start(f32[64,1280]{1,0:T(8,128)S(1)} %get-tuple-element.35.refs_9_), channel_id=1, source_target_pairs={{0,2},{25,27},{2,0},{27,25},{4,6},{29,23},{6,4},{23,29},{8,10},{17... | collective-permute-start | bytes 983048 | tf_op jit(solution)/shard_map/ppermute | solution.py:436
  40.5 23.3 %collective-permute-start.11 = (f32[64,1280]{1,0:T(8,128)S(1)}, f32[64,1280]{1,0:T(8,128)S(1)}, u32[]{:S(2)}, u32[]{:S(2)}) collective-permute-start(f32[64,1280]{1,0:T(8,128)S(1)} %get-tuple-element.37.refs_11_), channel_id=1, source_target_pairs={{22,20},{7,13},{24,26},{1,3},{26,24},{3,1},{28,30},{5,31},{30,28},... | collective-permute-start | bytes 983048 | tf_op jit(solution)/shard_map/ppermute | solution.py:436
  47.1 8.4 %collective-permute-start.8 = (f32[64,1024]{1,0:T(8,128)S(1)}, f32[64,1024]{1,0:T(8,128)S(1)}, u32[]{:S(2)}, u32[]{:S(2)}) collective-permute-start(f32[64,1024]{1,0:T(8,128)S(1)} %get-tuple-element.34.refs_8_), channel_id=1, source_target_pairs={{24,22},{1,7},{26,28},{3,5},{28,26},{5,3},{30,31},{31,30}} | collective-permute-start | bytes 786440 | tf_op jit(solution)/shard_map/ppermute | solution.py:436
  74.4 28.3 %collective-permute-start.12 = (f32[64,2304]{1,0:T(8,128)S(1)}, f32[64,2304]{1,0:T(8,128)S(1)}, u32[]{:S(2)}, u32[]{:S(2)}) collective-permute-start(f32[64,2304]{1,0:T(8,128)S(1)} %get-tuple-element.38), channel_id=1, source_target_pairs={{0,0},{25,2},{2,1},{27,4},{4,3},{29,6},{6,5},{23,8},{8,7},{17,10},... | collective-permute-start | bytes 1769480 | tf_op jit(solution)/shard_map/ppermute | solution.py:461
  76.3 26.4 %collective-permute-start.15 = (f32[64,2304]{1,0:T(8,128)S(1)}, f32[64,2304]{1,0:T(8,128)S(1)}, u32[]{:S(2)}, u32[]{:S(2)}) collective-permute-start(f32[64,2304]{1,0:T(8,128)S(1)} %get-tuple-element.41), channel_id=1, source_target_pairs={{0,1},{25,0},{2,3},{27,2},{4,5},{29,4},{6,7},{23,6},{8,9},{17,8},{... | collective-permute-start | bytes 1769480 | tf_op jit(solution)/shard_map/ppermute | solution.py:461
  76.4 26.3 %collective-permute-start.16 = (f32[64,1792]{1,0:T(8,128)S(1)}, f32[64,1792]{1,0:T(8,128)S(1)}, u32[]{:S(2)}, u32[]{:S(2)}) collective-permute-start(f32[64,1792]{1,0:T(8,128)S(1)} %get-tuple-element.42), channel_id=1, source_target_pairs={{16,17},{9,16},{18,19},{11,18},{20,21},{13,20},{22,23},{7,22},{24,... | collective-permute-start | bytes 1376264 | tf_op jit(solution)/shard_map/ppermute | solution.py:461
  79.9 12.5 %collective-permute-start.13 = (f32[64,1024]{1,0:T(8,128)S(1)}, f32[64,1024]{1,0:T(8,128)S(1)}, u32[]{:S(2)}, u32[]{:S(2)}) collective-permute-start(f32[64,1024]{1,0:T(8,128)S(1)} %get-tuple-element.39), channel_id=1, source_target_pairs={{16,15},{9,18},{18,17},{11,20},{20,19},{13,22},{22,21},{7,24},{24,... | collective-permute-start | bytes 786440 | tf_op jit(solution)/shard_map/ppermute | solution.py:461
  81.9 10.6 %collective-permute-start.14 = (f32[64,768]{1,0:T(8,128)S(1)}, f32[64,768]{1,0:T(8,128)S(1)}, u32[]{:S(2)}, u32[]{:S(2)}) collective-permute-start(f32[64,768]{1,0:T(8,128)S(1)} %get-tuple-element.40), channel_id=1, source_target_pairs={{24,23},{1,26},{26,25},{3,28},{28,27},{5,30},{30,29},{31,31}} | collective-permute-start | bytes 589832 | tf_op jit(solution)/shard_map/ppermute | solution.py:461
